TPU v7x, 128 devices: a whole 4x4x4 slice. The times are simulated.
128 devices in a mesh: site: 4 (over x), bond: 32 (over z, y, core).
Axes of the slice: x: 4, y: 4, z: 4, core: 2. Of those that a mesh axis runs over, the one named last changes fastest.
Arguments:
- start_rows: bfloat16 [1024, 4096], P(None, 'bond'), may hold values from -6 to 6
- site_tensors: bfloat16 [4, 4096, 8, 4096], P('site', None, None, 'bond'), may hold values from -0.09375 to 0.09375
- block_scales: float32 [4, 8, 32], P('site', None, 'bond'), may hold values from 0.25 to 1
- displacement: float32 [4, 8, 8], P('site'), may hold values from -0.9 to 0.9
- outcomes: int32 [4, 1024], P('site'), may hold values from 0 to 7
Outputs:
- leaving: bfloat16 [4, 1024, 4096], P('site', None, 'bond')
- log_norms: float32 [4, 1024], P('site')
Inputs may be any that keep to these rules, and one draw needn't show every extreme that they name: outcomes index the second dimension of displacement.
All inputs are finite; a program needn't handle non-finite values.
Results may differ from a plain program's by a relative error of at most 0.014.
Values may be sent and summed in bfloat16 or wider, within the bound.
No kernel may reach another device: no remote copies, remote signals or barrier semaphores. Data moves between devices by JAX's collectives and lax.ppermute only.
A program may use at most 64 MiB of HBM per device.

v0:
```python
import jax
import jax.numpy as jnp
from jax import lax
from jax.sharding import PartitionSpec as P

ROWS = 512


def shifted(value, axis, steps):
    count = lax.axis_size(axis)
    initial, last = (max(0, -steps), min(count, count - steps))
    return lax.ppermute(value, axis, [(source, source + steps) for source in range(initial, last)])


def local(start_rows, site_tensors, block_scales, displacement, outcomes):
    sites = lax.axis_size("site")
    cols = site_tensors.shape[3]
    chi = site_tensors.shape[1]
    phys = site_tensors.shape[2]
    nblk = block_scales.shape[2]
    allrows = start_rows.shape[0]
    grows = ROWS
    ngroups = allrows // grows
    ticks = ngroups + sites - 1
    a_mat = site_tensors[0].reshape(chi, phys * cols)
    scales = block_scales[0][:, :, None]
    table = displacement[0]
    outcome_row = outcomes[0]
    position = lax.axis_index("site")

    def tick(step, carry):
        incoming, incoming_norm, out_leave, out_logs = carry
        batch = step - position
        valid = jnp.logical_and(batch >= 0, batch < ngroups)
        first = jnp.clip(batch, 0, ngroups - 1) * grows
        start_piece = lax.dynamic_slice_in_dim(start_rows, first, grows, 0)
        rows_in = jnp.where(position == 0, start_piece, incoming)
        piece = lax.all_gather(rows_in, "bond", axis=1, tiled=True)
        total = jnp.dot(piece, a_mat, preferred_element_type=jnp.float32)
        pf = piece.astype(jnp.float32)
        total, squares = (total, jnp.sum(pf * pf, axis=1))
        local_norm = jnp.sqrt(squares / chi + 1e-06)
        norm = jnp.where(position == 0, local_norm, incoming_norm)
        prod = total.reshape(grows, phys, nblk, cols // nblk) * scales[None]
        prod = prod.reshape(grows, phys, cols)
        picked = lax.dynamic_slice_in_dim(outcome_row, first, grows, 0)
        onehot = (picked[:, None] == jnp.arange(phys, dtype=jnp.int32)[None, :]).astype(jnp.float32)
        weight = jnp.dot(onehot, table, precision=lax.Precision.HIGHEST)
        mixed = jnp.sum(weight[:, :, None] * prod, axis=1)
        leave = (mixed / norm[:, None]).astype(jnp.bfloat16)
        out_leave = jnp.where(
            valid, lax.dynamic_update_slice_in_dim(out_leave, leave, first, 0), out_leave
        )
        out_logs = jnp.where(
            valid, lax.dynamic_update_slice_in_dim(out_logs, jnp.log(norm), first, 0), out_logs
        )
        lf = leave.astype(jnp.float32)
        sent_sq = lax.psum(jnp.sum(lf * lf, axis=1), "bond")
        sent_norm = jnp.sqrt(sent_sq / chi + 1e-06)
        incoming, incoming_norm = (
            shifted(leave, "site", 1),
            shifted(sent_norm.astype(jnp.bfloat16), "site", 1).astype(sent_norm.dtype),
        )
        return (incoming, incoming_norm, out_leave, out_logs)

    carry = (
        jnp.zeros((grows, cols), jnp.bfloat16),
        jnp.ones((grows,), jnp.float32),
        jnp.zeros((allrows, cols), jnp.bfloat16),
        jnp.zeros((allrows,), jnp.float32),
    )
    carry = lax.fori_loop(0, ticks, tick, carry)
    return (carry[2][None], carry[3][None])


def solution(mesh):
    return jax.shard_map(
        local,
        mesh=mesh,
        in_specs=(
            P(None, "bond"),
            P("site", None, None, "bond"),
            P("site", None, "bond"),
            P("site", None, None),
            P("site", None),
        ),
        out_specs=(P("site", None, "bond"), P("site", None)),
        check_vma=False,
    )
```

profile of v0, /device:TPU:1, one launch (start us, length us, event | category | flops | bytes accessed | tf_op | source)
XLA Modules:
  0.0 702.8 jit_solution(6825143488463215388)
XLA Ops:
  7.2 8.8 %copy.12 = bf16[512,8,8,128]{3,1,2,0:T(8,128)(2,1)} copy(bf16[512,8,8,128]{3,2,1,0:T(8,128)(2,1)} %bitcast.33) | data formatting | bytes 16777216
  16.1 679.4 %while.21 = (s32[]{:T(128)}, bf16[512,128]{1,0:T(8,128)(2,1)S(1)}, f32[512]{0:T(512)S(1)}, bf16[1024,128]{1,0:T(8,128)(2,1)S(1)}, f32[1024]{0:T(1024)S(1)}, /*in...) while((s32[]{:T(128)}, bf16[512,128]{1,0:T(8,128)(2,1)S(1)}, ...), condition=%wide.region_5.6_spmd.clone, body=%wide.region_0.5_spmd.clone.sunk | while | flops 4303626240 | bytes 56955604 | solution.py:72
  17.4 55.5 %all-gather.2.cloned.1.call-done = bf16[512,4096]{1,0:T(8,128)(2,1)} async-done(((bf16[512,128]{1,0:T(8,128)(2,1)}), bf16[512,4096]{1,0:T(8,128)(2,1)}) %all-gather.2.cloned.1.call-update) | async-done | bytes 4194320 | tf_op jit(solution)/shard_map/while/body/eval_jaxpr/all_gather | solution.py:38
  72.8 8.1 %convolution_bitcast_fusion.2 = f32[64,8,8,128]{3,1,2,0:T(8,128)S(1)} fusion(bf16[512,4096]{1,0:T(8,128)(2,1)} %all-gather.2.cloned.1.call-done, bf16[4096,1024]{1,0:T(8,128)(2,1)} %get-tuple-element.430), kind=kOutput, calls=%fused_computation.4.clone.1 | convolution fusion | flops 4294967296 | bytes 14680064 | tf_op jit(solution)/shard_map/while/body/eval_jaxpr/dot_general | solution.py:39
  81.5 2.5 fusion.16
  85.2 3.1 collective-permute-start
  88.5 62.6 %psum.14 = f32[512]{0:T(512)S(1)} all-reduce(f32[512]{0:T(512)S(1)} %multiply_reduce_fusion.5), channel_id=1, replica_groups=mesh['site'=4,'bond'=32] {'bond'}, use_global_device_ids=true, to_apply=%region_4.4 | all-reduce | flops 512 | bytes 4096 | tf_op jit(solution)/shard_map/while/body/eval_jaxpr/psum | solution.py:58
  151.0 3.1 collective-permute-start.1
  156.0 52.2 %all-gather.2.cloned.1.call-done = bf16[512,4096]{1,0:T(8,128)(2,1)} async-done(((bf16[512,128]{1,0:T(8,128)(2,1)}), bf16[512,4096]{1,0:T(8,128)(2,1)}) %all-gather.2.cloned.1.call-update) | async-done | bytes 4194320 | tf_op jit(solution)/shard_map/while/body/eval_jaxpr/all_gather | solution.py:38
  208.2 8.1 %convolution_bitcast_fusion.2 = f32[64,8,8,128]{3,1,2,0:T(8,128)S(1)} fusion(bf16[512,4096]{1,0:T(8,128)(2,1)} %all-gather.2.cloned.1.call-done, bf16[4096,1024]{1,0:T(8,128)(2,1)} %get-tuple-element.430), kind=kOutput, calls=%fused_computation.4.clone.1 | convolution fusion | flops 4294967296 | bytes 14680064 | tf_op jit(solution)/shard_map/while/body/eval_jaxpr/dot_general | solution.py:39
  216.8 2.5 fusion.16
  220.5 3.1 collective-permute-start
  223.8 62.6 %psum.14 = f32[512]{0:T(512)S(1)} all-reduce(f32[512]{0:T(512)S(1)} %multiply_reduce_fusion.5), channel_id=1, replica_groups=mesh['site'=4,'bond'=32] {'bond'}, use_global_device_ids=true, to_apply=%region_4.4 | all-reduce | flops 512 | bytes 4096 | tf_op jit(solution)/shard_map/while/body/eval_jaxpr/psum | solution.py:58
  286.4 3.1 collective-permute-start.1
  291.3 52.2 %all-gather.2.cloned.1.call-done = bf16[512,4096]{1,0:T(8,128)(2,1)} async-done(((bf16[512,128]{1,0:T(8,128)(2,1)}), bf16[512,4096]{1,0:T(8,128)(2,1)}) %all-gather.2.cloned.1.call-update) | async-done | bytes 4194320 | tf_op jit(solution)/shard_map/while/body/eval_jaxpr/all_gather | solution.py:38
  343.5 8.1 %convolution_bitcast_fusion.2 = f32[64,8,8,128]{3,1,2,0:T(8,128)S(1)} fusion(bf16[512,4096]{1,0:T(8,128)(2,1)} %all-gather.2.cloned.1.call-done, bf16[4096,1024]{1,0:T(8,128)(2,1)} %get-tuple-element.430), kind=kOutput, calls=%fused_computation.4.clone.1 | convolution fusion | flops 4294967296 | bytes 14680064 | tf_op jit(solution)/shard_map/while/body/eval_jaxpr/dot_general | solution.py:39
  352.1 2.5 fusion.16
  355.9 3.1 collective-permute-start
  359.1 62.6 %psum.14 = f32[512]{0:T(512)S(1)} all-reduce(f32[512]{0:T(512)S(1)} %multiply_reduce_fusion.5), channel_id=1, replica_groups=mesh['site'=4,'bond'=32] {'bond'}, use_global_device_ids=true, to_apply=%region_4.4 | all-reduce | flops 512 | bytes 4096 | tf_op jit(solution)/shard_map/while/body/eval_jaxpr/psum | solution.py:58
  421.7 3.1 collective-permute-start.1
  426.6 51.9 %all-gather.2.cloned.1.call-done = bf16[512,4096]{1,0:T(8,128)(2,1)} async-done(((bf16[512,128]{1,0:T(8,128)(2,1)}), bf16[512,4096]{1,0:T(8,128)(2,1)}) %all-gather.2.cloned.1.call-update) | async-done | bytes 4194320 | tf_op jit(solution)/shard_map/while/body/eval_jaxpr/all_gather | solution.py:38
  478.5 8.1 %convolution_bitcast_fusion.2 = f32[64,8,8,128]{3,1,2,0:T(8,128)S(1)} fusion(bf16[512,4096]{1,0:T(8,128)(2,1)} %all-gather.2.cloned.1.call-done, bf16[4096,1024]{1,0:T(8,128)(2,1)} %get-tuple-element.430), kind=kOutput, calls=%fused_computation.4.clone.1 | convolution fusion | flops 4294967296 | bytes 14680064 | tf_op jit(solution)/shard_map/while/body/eval_jaxpr/dot_general | solution.py:39
  487.1 2.5 fusion.16
  490.9 3.1 collective-permute-start
  494.1 62.6 %psum.14 = f32[512]{0:T(512)S(1)} all-reduce(f32[512]{0:T(512)S(1)} %multiply_reduce_fusion.5), channel_id=1, replica_groups=mesh['site'=4,'bond'=32] {'bond'}, use_global_device_ids=true, to_apply=%region_4.4 | all-reduce | flops 512 | bytes 4096 | tf_op jit(solution)/shard_map/while/body/eval_jaxpr/psum | solution.py:58
  556.7 3.1 collective-permute-start.1
  561.7 51.9 %all-gather.2.cloned.1.call-done = bf16[512,4096]{1,0:T(8,128)(2,1)} async-done(((bf16[512,128]{1,0:T(8,128)(2,1)}), bf16[512,4096]{1,0:T(8,128)(2,1)}) %all-gather.2.cloned.1.call-update) | async-done | bytes 4194320 | tf_op jit(solution)/shard_map/while/body/eval_jaxpr/all_gather | solution.py:38
  613.5 8.1 %convolution_bitcast_fusion.2 = f32[64,8,8,128]{3,1,2,0:T(8,128)S(1)} fusion(bf16[512,4096]{1,0:T(8,128)(2,1)} %all-gather.2.cloned.1.call-done, bf16[4096,1024]{1,0:T(8,128)(2,1)} %get-tuple-element.430), kind=kOutput, calls=%fused_computation.4.clone.1 | convolution fusion | flops 4294967296 | bytes 14680064 | tf_op jit(solution)/shard_map/while/body/eval_jaxpr/dot_general | solution.py:39
  622.2 2.5 fusion.16
  625.9 3.1 collective-permute-start
  629.2 62.6 %psum.14 = f32[512]{0:T(512)S(1)} all-reduce(f32[512]{0:T(512)S(1)} %multiply_reduce_fusion.5), channel_id=1, replica_groups=mesh['site'=4,'bond'=32] {'bond'}, use_global_device_ids=true, to_apply=%region_4.4 | all-reduce | flops 512 | bytes 4096 | tf_op jit(solution)/shard_map/while/body/eval_jaxpr/psum | solution.py:58
  691.7 3.1 collective-permute-start.1
  (96 shorter events, 19.3 us)
Async XLA Ops:
  7.2 8.9 %copy-start.2 = (bf16[1024,128]{1,0:T(8,128)(2,1)S(1)}, bf16[1024,128]{1,0:T(8,128)(2,1)}, u32[]{:S(2)}) copy-start(bf16[1024,128]{1,0:T(8,128)(2,1)} %param.7) | copy-start | bytes 786436
  7.2 8.9 %copy-start.3 = (f32[1,8,8]{2,1,0:T(8,128)S(1)}, f32[1,8,8]{2,1,0:T(8,128)}, u32[]{:S(2)}) copy-start(f32[1,8,8]{2,1,0:T(8,128)} %param.10) | copy-start | bytes 772
  7.2 8.9 %copy-start.5 = (s32[1,1024]{1,0:T(1,128)S(1)}, s32[1,1024]{1,0:T(1,128)}, u32[]{:S(2)}) copy-start(s32[1,1024]{1,0:T(1,128)} %param.11) | copy-start | bytes 12292
  7.2 8.9 %copy-start.6 = (f32[1,8,1]{1,2,0:T(1,128)S(1)}, f32[1,8,1]{1,2,0:T(1,128)}, u32[]{:S(2)}) copy-start(f32[1,8,1]{1,2,0:T(1,128)} %param.9) | copy-start | bytes 100
  16.1 56.7 %all-gather.2.cloned.1.call-start = ((), (), s32[]{:S(2)}) async-start(), calls=%async_computation | async-start | bytes 4325376 | tf_op jit(solution)/shard_map/while/body/eval_jaxpr/all_gather | solution.py:38
  81.0 3.0 copy-start
  85.2 69.6 %collective-permute-start = (bf16[512,128]{1,0:T(8,128)(2,1)S(1)}, bf16[512,128]{1,0:T(8,128)(2,1)S(1)}, u32[]{:S(2)}, u32[]{:S(2)}) collective-permute-start(bf16[512,128]{1,0:T(8,128)(2,1)S(1)} %get-tuple-element.383), channel_id=1, source_target_pairs={{0,32},{32,64},{64,96},{1,33},{33,65},{65,97},{2,34},{34,66},{66,9... | collective-permute-start | bytes 393224 | tf_op jit(solution)/shard_map/while/body/eval_jaxpr/ppermute | solution.py:12
  151.0 3.8 collective-permute-start.1
  154.8 53.3 %all-gather.2.cloned.1.call-start = ((), (), s32[]{:S(2)}) async-start(), calls=%async_computation | async-start | bytes 4325376 | tf_op jit(solution)/shard_map/while/body/eval_jaxpr/all_gather | solution.py:38
  216.3 3.0 copy-start
  220.5 69.6 %collective-permute-start = (bf16[512,128]{1,0:T(8,128)(2,1)S(1)}, bf16[512,128]{1,0:T(8,128)(2,1)S(1)}, u32[]{:S(2)}, u32[]{:S(2)}) collective-permute-start(bf16[512,128]{1,0:T(8,128)(2,1)S(1)} %get-tuple-element.383), channel_id=1, source_target_pairs={{0,32},{32,64},{64,96},{1,33},{33,65},{65,97},{2,34},{34,66},{66,9... | collective-permute-start | bytes 393224 | tf_op jit(solution)/shard_map/while/body/eval_jaxpr/ppermute | solution.py:12
  286.4 3.8 collective-permute-start.1
  290.2 53.3 %all-gather.2.cloned.1.call-start = ((), (), s32[]{:S(2)}) async-start(), calls=%async_computation | async-start | bytes 4325376 | tf_op jit(solution)/shard_map/while/body/eval_jaxpr/all_gather | solution.py:38
  351.6 3.0 copy-start
  355.9 69.6 %collective-permute-start = (bf16[512,128]{1,0:T(8,128)(2,1)S(1)}, bf16[512,128]{1,0:T(8,128)(2,1)S(1)}, u32[]{:S(2)}, u32[]{:S(2)}) collective-permute-start(bf16[512,128]{1,0:T(8,128)(2,1)S(1)} %get-tuple-element.383), channel_id=1, source_target_pairs={{0,32},{32,64},{64,96},{1,33},{33,65},{65,97},{2,34},{34,66},{66,9... | collective-permute-start | bytes 393224 | tf_op jit(solution)/shard_map/while/body/eval_jaxpr/ppermute | solution.py:12
  421.7 3.8 collective-permute-start.1
  425.5 53.0 %all-gather.2.cloned.1.call-start = ((), (), s32[]{:S(2)}) async-start(), calls=%async_computation | async-start | bytes 4325376 | tf_op jit(solution)/shard_map/while/body/eval_jaxpr/all_gather | solution.py:38
  486.6 3.0 copy-start
  490.9 69.6 %collective-permute-start = (bf16[512,128]{1,0:T(8,128)(2,1)S(1)}, bf16[512,128]{1,0:T(8,128)(2,1)S(1)}, u32[]{:S(2)}, u32[]{:S(2)}) collective-permute-start(bf16[512,128]{1,0:T(8,128)(2,1)S(1)} %get-tuple-element.383), channel_id=1, source_target_pairs={{0,32},{32,64},{64,96},{1,33},{33,65},{65,97},{2,34},{34,66},{66,9... | collective-permute-start | bytes 393224 | tf_op jit(solution)/shard_map/while/body/eval_jaxpr/ppermute | solution.py:12
  556.7 3.8 collective-permute-start.1
  560.5 53.0 %all-gather.2.cloned.1.call-start = ((), (), s32[]{:S(2)}) async-start(), calls=%async_computation | async-start | bytes 4325376 | tf_op jit(solution)/shard_map/while/body/eval_jaxpr/all_gather | solution.py:38
  621.7 3.0 copy-start
  625.9 69.6 %collective-permute-start = (bf16[512,128]{1,0:T(8,128)(2,1)S(1)}, bf16[512,128]{1,0:T(8,128)(2,1)S(1)}, u32[]{:S(2)}, u32[]{:S(2)}) collective-permute-start(bf16[512,128]{1,0:T(8,128)(2,1)S(1)} %get-tuple-element.383), channel_id=1, source_target_pairs={{0,32},{32,64},{64,96},{1,33},{33,65},{65,97},{2,34},{34,66},{66,9... | collective-permute-start | bytes 393224 | tf_op jit(solution)/shard_map/while/body/eval_jaxpr/ppermute | solution.py:12
  691.7 3.8 collective-permute-start.1
  695.5 0.7 copy-start.1
  695.5 0.7 copy-start.4
Sparse Core Ops, SparseCore 0:
  19.7 53.0 all-gather.1
  158.4 49.6 all-gather.1
  293.7 49.6 all-gather.1
  428.8 49.6 all-gather.1
  563.8 49.6 all-gather.1
where the time goes:
time: 706 us; the launch traced here: 703 us
  blocking collectives  313 us (44%)
  waiting for transfers between devices  267 us (38%)
  matrix products  42.3 us (6%)
  starting transfers between devices  31 us (4%)
  other arithmetic  22.9 us (3%)
  between operations  13.8 us (2%)
  local copies, waits for them, and re-layouts  12.3 us (2%)
    psum x5, blocking collectives, tick(): sent_sq = lax.psum(jnp.sum(lf * lf, axis=1), 'bond')  313 us
    all_gather x5, waiting for transfers between devices, tick(): piece = lax.all_gather(rows_in, 'bond', axis=1, tiled=True)  263 us
    dot_general x5, matrix products, tick(): total = jnp.dot(piece, a_mat, preferred_element_type=jnp.float32)  40.7 us
    ppermute x10, starting transfers between devices, shifted(): lax.ppermute(value, axis, [(source, source + steps) for source in range(i...  30.9 us
  transfers between devices with their start and end apart: 15, of which 10 were waited for; matrix products, arithmetic and copies ran while one was open for 0% of the time, Pallas kernels for 0%

commit v1 on v0

v1 whole, which is shorter than its diff:
```python
import functools

import jax
import jax.numpy as jnp
from jax import lax
from jax.experimental import pallas as pl
from jax.experimental.pallas import tpu as pltpu
from jax.sharding import Mesh, PartitionSpec as P

ROWS = 256
NZ, NY, NC = 4, 4, 2
BOND = ("z", "y", "core")


def contract_kernel(y_ref, x_ref, w_ref, own_ref, part_ref, mixed_ref, other_ref):
    phys = w_ref.shape[0]
    y = y_ref[0]
    blocks = []
    for z in range(NZ):
        for yy in range(NY):
            blocks.append(x_ref[z, lax.rem(y - yy + NY, NY)])
    rows = jnp.concatenate(blocks, axis=1)
    cols = mixed_ref.shape[1]
    squares = None
    for block in blocks:
        wide = block.astype(jnp.float32)
        squares = wide * wide if squares is None else squares + wide * wide
    mixed = jnp.zeros(mixed_ref.shape, jnp.float32)
    other = jnp.zeros(mixed_ref.shape, jnp.float32)
    for p in range(phys):
        prod = jnp.dot(rows, w_ref[p], preferred_element_type=jnp.float32)
        mixed += own_ref[:, p : p + 1] * prod[:, :cols]
        other += part_ref[:, p : p + 1] * prod[:, cols:]
    total = jnp.broadcast_to(jnp.sum(squares, axis=1, keepdims=True), mixed_ref.shape)
    mixed_ref[...] = mixed
    other_ref[:, :cols] = other
    other_ref[:, cols:] = total


def contract(y, x, w, own, part):
    rows, cols = x.shape[2], x.shape[3]
    vmem = pl.BlockSpec(memory_space=pltpu.VMEM)
    return pl.pallas_call(
        contract_kernel,
        out_shape=(
            jax.ShapeDtypeStruct((rows, cols), jnp.float32),
            jax.ShapeDtypeStruct((rows, 2 * cols), jnp.float32),
        ),
        in_specs=[pl.BlockSpec(memory_space=pltpu.SMEM)] + [vmem] * 4,
        out_specs=(vmem, vmem),
        compiler_params=pltpu.CompilerParams(vmem_limit_bytes=24 * 2**20),
    )(y, x, w, own, part)


def local(start_rows, site_tensors, block_scales, displacement, outcomes):
    sites = lax.axis_size("site")
    chi, phys, cols = site_tensors.shape[1:]
    allrows = start_rows.shape[0]
    ngroups = allrows // ROWS
    ticks = ngroups + sites - 1
    position = lax.axis_index("site")
    core = lax.axis_index("core")
    y = lax.axis_index("y")
    swap = [(0, 1), (1, 0)]

    def to_partner(value):
        return lax.ppermute(value, "core", swap)

    def diagonals(value):
        return jnp.stack([
            lax.ppermute(
                value,
                ("site", "y"),
                [
                    (s * NY + q, ((s + 1) % sites) * NY + (q + shift) % NY)
                    for s in range(sites)
                    for q in range(NY)
                ],
            )
            for shift in range(NY)
        ])

    def along_z(value):
        return lax.all_to_all(jnp.broadcast_to(value[None], (NZ,) + value.shape), "z", 0, 0)

    def start_piece(batch):
        return start_rows[batch * ROWS : (batch + 1) * ROWS]

    tensor = site_tensors[0].reshape(chi // (NC * cols), NC, cols, phys, cols)
    keep = lax.dynamic_index_in_dim(tensor, core, 1, keepdims=False)
    give = lax.dynamic_index_in_dim(tensor, 1 - core, 1, keepdims=False)
    got = to_partner(give)
    half = chi // NC
    w = jnp.concatenate(
        [jnp.swapaxes(part.reshape(half, phys, cols), 0, 1) for part in (keep, got)], axis=2
    )
    scale = block_scales[0][:, 0]
    partner_scale = to_partner(scale)
    onehot = (outcomes[0][:, None] == jnp.arange(phys, dtype=jnp.int32)[None, :]).astype(jnp.float32)
    weight = jnp.dot(onehot, displacement[0], precision=lax.Precision.HIGHEST)
    own_coef = weight * scale[None, :]
    part_coef = weight * partner_scale[None, :]
    y_arr = y[None].astype(jnp.int32)

    gathered = along_z(diagonals(start_piece(0)))
    leaves, logs = [], []
    for step in range(ticks):
        batch = jnp.clip(step - position, 0, ngroups - 1)
        first = batch * ROWS
        own = lax.dynamic_slice_in_dim(own_coef, first, ROWS, 0)
        part = lax.dynamic_slice_in_dim(part_coef, first, ROWS, 0)
        mixed, other = contract(y_arr, gathered, w, own, part)
        arrived = to_partner(other)
        norm = jnp.sqrt((other[:, cols:] + arrived[:, cols:]) / chi + 1e-06)
        leave = ((mixed + arrived[:, :cols]) / norm).astype(jnp.bfloat16)
        leaves.append(leave)
        logs.append(jnp.log(norm[:, 0]))
        if step + 1 < ticks:
            ahead = start_piece(min(step + 1, ngroups - 1))
            gathered = along_z(diagonals(jnp.where(position == sites - 1, ahead, leave)))
    out_leave = lax.dynamic_slice_in_dim(jnp.concatenate(leaves, 0), position * ROWS, allrows, 0)
    out_logs = lax.dynamic_slice_in_dim(jnp.concatenate(logs, 0), position * ROWS, allrows, 0)
    return (out_leave[None], out_logs[None])


def solution(mesh):
    fine = Mesh(mesh.devices.reshape(-1, NZ, NY, NC), ("site",) + BOND)
    return jax.shard_map(
        local,
        mesh=fine,
        in_specs=(
            P(None, BOND),
            P("site", None, None, BOND),
            P("site", None, BOND),
            P("site", None, None),
            P("site", None),
        ),
        out_specs=(P("site", None, BOND), P("site", None)),
        check_vma=False,
    )
```

time: 706 us -> 265 us (0.38)
  blocking collectives: 313 us -> 62.7 us
  waiting for transfers between devices: 267 us -> 67.7 us
  matrix products: 42.3 us -> 0.46 us
  starting transfers between devices: 31 us -> 72.1 us
  local copies, waits for them, and re-layouts: 12.3 us -> 35 us
  Pallas kernels: 0 us -> 17.4 us
  other arithmetic: 22.9 us -> 8.54 us
  between operations: 13.8 us -> 0.93 us
    psum x5 -> x0, blocking collectives: 313 us -> none  [tick(): sent_sq = lax.psum(jnp.sum(lf * lf, axis=1), 'bond')]
    all_gather x5 -> x0, waiting for transfers between devices: 263 us -> none  [tick(): piece = lax.all_gather(rows_in, 'bond', axis=1, tiled=True)]
    all_to_all x0 -> x4, blocking collectives: none -> 62.7 us  [along_z(): lax.all_to_all(jnp.broadcast_to(value[None], (NZ,) + value.shape), 'z', 0...]
    dot_general x10 -> x1, matrix products: 42.3 us -> 0.46 us  [local(): weight = jnp.dot(onehot, displacement[0], precision=lax.Precision.HIGHEST)]
    ppermute x10 -> x37, waiting for transfers between devices: 3.55 us -> 35.9 us  [the longest x28 28 us: diagonals(): lax.ppermute(value, ('site', 'y'), [(s * NY + q, (s + 1) % sites * NY + (...]
    all_to_all x0 -> x3, waiting for transfers between devices: none -> 31.8 us  [along_z(): lax.all_to_all(jnp.broadcast_to(value[None], (NZ,) + value.shape), 'z', 0...]
    ppermute x10 -> x37, starting transfers between devices: 30.9 us -> 60.1 us  [the longest x28 38.3 us: diagonals(): lax.ppermute(value, ('site', 'y'), [(s * NY + q, (s + 1) % sites * NY + (...]
    reduce_sum x15 -> x0, other arithmetic: 17.6 us -> none  [the longest x5 12.4 us: tick(): mixed = jnp.sum(weight[:, :, None] * prod, axis=1)]
  transfers between devices with their start and end apart: 15 -> 40, of which waited for: 10 -> 29; matrix products, arithmetic and copies ran while one was open for 0% -> 6% of each run, Pallas kernels for 0% -> 0%
where the time goes in v1:
time: 265 us
  starting transfers between devices  72.1 us (27%)
  waiting for transfers between devices  67.7 us (26%)
  blocking collectives  62.7 us (24%)
  local copies, waits for them, and re-layouts  35 us (13%)
  Pallas kernels  17.4 us (7%)
  other arithmetic  8.54 us (3%)
    all_to_all x4, blocking collectives, along_z(): lax.all_to_all(jnp.broadcast_to(value[None], (NZ,) + value.shape), 'z', 0...  62.7 us
    ppermute x28, starting transfers between devices, diagonals(): lax.ppermute(value, ('site', 'y'), [(s * NY + q, (s + 1) % sites * NY + (...  38.3 us
    all_to_all x3, waiting for transfers between devices, along_z(): lax.all_to_all(jnp.broadcast_to(value[None], (NZ,) + value.shape), 'z', 0...  31.8 us
    ppermute x28, waiting for transfers between devices, diagonals(): lax.ppermute(value, ('site', 'y'), [(s * NY + q, (s + 1) % sites * NY + (...  28 us
    ppermute x9, starting transfers between devices, to_partner(): return lax.ppermute(value, 'core', swap)  21.7 us
    unnamed x29, local copies, waits for them, and re-layouts  18.9 us
    pallas_call x7, Pallas kernels, contract(): pl.pallas_call(contract_kernel, out_shape=(jax.ShapeDtypeStruct((rows, co...  17.4 us
    all_to_all x3, starting transfers between devices, along_z(): lax.all_to_all(jnp.broadcast_to(value[None], (NZ,) + value.shape), 'z', 0...  12.1 us
  transfers between devices with their start and end apart: 40, of which 29 were waited for; matrix products, arithmetic and copies ran while one was open for 6% of the time, Pallas kernels for 0%

profile of v1, /device:TPU:1, one launch (start us, length us, event | category | flops | bytes accessed | tf_op | source)
XLA Modules:
  0.0 264.7 jit_solution(4703863455899373367)
XLA Ops:
  0.6 6.3 %constant_dynamic-slice_fusion.15 = (bf16[16,1,128,8,128]{4,3,2,1,0:T(8,128)(2,1)}, bf16[16,1,128,8,128]{4,3,2,1,0:T(8,128)(2,1)S(1)}) fusion(bf16[16,2,128,8,128]{4,3,2,1,0:T(8,128)(2,1)} %bitcast.50, s32[]{:T(128)S(6)} %select_n.67, s32[]{:T(128)S(6)} %select_n.68), kind=kLoop, calls=%fused_computation.113 | loop fusion | bytes 16777224 | tf_op jit(solution)/shard_map/jit(dynamic_index_in_dim)/dynamic_slice | solution.py:90
  6.9 3.1 %copy.18 = bf16[16,1,128,8,128]{4,2,0,3,1:T(8,128)(2,1)} copy(bf16[16,1,128,8,128]{4,3,2,1,0:T(8,128)(2,1)S(1)} %get-tuple-element.51) | data formatting | bytes 8388608 | tf_op jit(solution)/shard_map/jit(dynamic_index_in_dim)/dynamic_slice | solution.py:91
  11.4 3.8 %collective-permute-start.3 = (bf16[256,128]{1,0:T(8,128)(2,1)S(1)}, bf16[256,128]{1,0:T(8,128)(2,1)S(1)}, u32[]{:S(2)}, u32[]{:S(2)}) collective-permute-start(bf16[256,128]{1,0:T(8,128)(2,1)S(1)} %slice.99), channel_id=1, source_target_pairs={{0,38},{2,32},{4,34},{6,36},{32,70},{34,64},{36,66},{38,68},{64,10... | collective-permute-start | bytes 196616 | tf_op jit(solution)/shard_map/ppermute | solution.py:71
  18.0 5.2 %copy.16 = bf16[16,1,128,8,128]{4,2,0,3,1:T(8,128)(2,1)} copy(bf16[16,1,128,8,128]{4,3,2,1,0:T(8,128)(2,1)} %get-tuple-element.50) | data formatting | bytes 8388608
  25.7 5.0 %all-to-all-start = ((bf16[4,4,256,128]{3,2,1,0:T(8,128)(2,1)}), bf16[4,4,256,128]{3,2,1,0:T(8,128)(2,1)S(1)}, u32[]{:S(2)}, u32[]{:S(2)}) async-start(bf16[4,4,256,128]{3,2,1,0:T(8,128)(2,1)} %broadcast_in_dim.21), calls=%async_computation | async-start | bytes 2097152 | tf_op jit(solution)/shard_map/all_to_all | solution.py:84
  31.4 7.7 %pad_maximum_fusion.w_ref = bf16[8,2048,256]{2,1,0:T(8,128)(2,1)} fusion(bf16[8,2048,128]{2,1,0:T(8,128)(2,1)} %bitcast.10, bf16[8,2048,128]{2,1,0:T(8,128)(2,1)} %bitcast.49), kind=kLoop, calls=%fused_computation | loop fusion | flops 16777216 | bytes 16777216 | tf_op jit(solution)/shard_map/concatenate | solution.py:94
  39.0 5.6 %all-to-all-done.x_ref = bf16[4,4,256,128]{3,2,1,0:T(8,128)(2,1)S(1)} async-done(((bf16[4,4,256,128]{3,2,1,0:T(8,128)(2,1)}), bf16[4,4,256,128]{3,2,1,0:T(8,128)(2,1)S(1)}, u32[]{:S(2)}, u32[]{:S(2)}) %all-to-all-start) | async-done | bytes 1048608 | tf_op jit(solution)/shard_map/all_to_all | solution.py:84
  44.7 3.4 %copy-done.1 = bf16[8,2048,256]{2,1,0:T(8,128)(2,1)S(1)} copy-done((bf16[8,2048,256]{2,1,0:T(8,128)(2,1)S(1)}, bf16[8,2048,256]{2,1,0:T(8,128)(2,1)}, u32[]{:S(2)}) %copy-start.1) | copy-done | bytes 8388632
  48.1 2.5 shard_map.68
  53.9 3.0 %collective-permute-start.10 = (bf16[256,128]{1,0:T(8,128)(2,1)S(1)}, bf16[256,128]{1,0:T(8,128)(2,1)S(1)}, u32[]{:S(2)}, u32[]{:S(2)}) collective-permute-start(bf16[256,128]{1,0:T(8,128)(2,1)S(1)} %get-tuple-element.47), channel_id=1, source_target_pairs={{0,38},{2,32},{4,34},{6,36},{32,70},{34,64},{36,66},{38,68},{64,10... | collective-permute-start | bytes 196616 | tf_op jit(solution)/shard_map/ppermute | solution.py:71
  60.2 3.5 %collective-permute-done.9 = bf16[256,128]{1,0:T(8,128)(2,1)S(1)} collective-permute-done((bf16[256,128]{1,0:T(8,128)(2,1)S(1)}, bf16[256,128]{1,0:T(8,128)(2,1)S(1)}, u32[]{:S(2)}, u32[]{:S(2)}) %collective-permute-start.9) | collective-permute-done | bytes 65568 | tf_op jit(solution)/shard_map/ppermute | solution.py:71
  66.2 15.2 %all_to_all.35.x_ref = bf16[4,4,256,128]{3,2,1,0:T(8,128)(2,1)S(1)} all-to-all(bf16[4,4,256,128]{3,2,1,0:T(8,128)(2,1)S(1)} %broadcast_in_dim.22), channel_id=1, replica_groups=mesh['site'=4,'z'=4,'y'=4,'core'=2] {'z'}, dimensions={0} | all-to-all | bytes 2097152 | tf_op jit(solution)/shard_map/all_to_all | solution.py:84
  81.4 3.4 %copy-done.2 = bf16[8,2048,256]{2,1,0:T(8,128)(2,1)S(1)} copy-done((bf16[8,2048,256]{2,1,0:T(8,128)(2,1)S(1)}, bf16[8,2048,256]{2,1,0:T(8,128)(2,1)}, u32[]{:S(2)}) %copy-start.2) | copy-done | bytes 8388632
  87.2 3.5 %collective-permute-start.11 = (f32[256,256]{1,0:T(8,128)S(1)}, f32[256,256]{1,0:T(8,128)S(1)}, u32[]{:S(2)}, u32[]{:S(2)}) collective-permute-start(f32[256,256]{1,0:T(8,128)S(1)} %get-tuple-element.19), channel_id=1, source_target_pairs={{0,1},{1,0},{2,3},{3,2},{4,5},{5,4},{6,7},{7,6},{8,9},{9,8},{10,11... | collective-permute-start | bytes 786440 | tf_op jit(solution)/shard_map/ppermute | solution.py:67
  102.2 16.3 %all_to_all.36.x_ref = bf16[4,4,256,128]{3,2,1,0:T(8,128)(2,1)S(1)} all-to-all(bf16[4,4,256,128]{3,2,1,0:T(8,128)(2,1)S(1)} %broadcast_in_dim.23), channel_id=1, replica_groups=mesh['site'=4,'z'=4,'y'=4,'core'=2] {'z'}, dimensions={0} | all-to-all | bytes 2097152 | tf_op jit(solution)/shard_map/all_to_all | solution.py:84
  118.5 2.5 shard_map.70
  134.1 15.9 %all_to_all.37.x_ref = bf16[4,4,256,128]{3,2,1,0:T(8,128)(2,1)S(1)} all-to-all(bf16[4,4,256,128]{3,2,1,0:T(8,128)(2,1)S(1)} %broadcast_in_dim.24), channel_id=1, replica_groups=mesh['site'=4,'z'=4,'y'=4,'core'=2] {'z'}, dimensions={0} | all-to-all | bytes 2097152 | tf_op jit(solution)/shard_map/all_to_all | solution.py:84
  152.5 2.7 %collective-permute-start.21 = (f32[256,256]{1,0:T(8,128)S(1)}, f32[256,256]{1,0:T(8,128)S(1)}, u32[]{:S(2)}, u32[]{:S(2)}) collective-permute-start(f32[256,256]{1,0:T(8,128)S(1)} %get-tuple-element.23), channel_id=1, source_target_pairs={{0,1},{1,0},{2,3},{3,2},{4,5},{5,4},{6,7},{7,6},{8,9},{9,8},{10,11... | collective-permute-start | bytes 786440 | tf_op jit(solution)/shard_map/ppermute | solution.py:67
  165.5 15.2 %all_to_all.38.x_ref = bf16[4,4,256,128]{3,2,1,0:T(8,128)(2,1)S(1)} all-to-all(bf16[4,4,256,128]{3,2,1,0:T(8,128)(2,1)S(1)} %broadcast_in_dim.25), channel_id=1, replica_groups=mesh['site'=4,'z'=4,'y'=4,'core'=2] {'z'}, dimensions={0} | all-to-all | bytes 2097152 | tf_op jit(solution)/shard_map/all_to_all | solution.py:84
  180.8 2.5 shard_map.72
  183.3 3.3 %collective-permute-start.26 = (f32[256,256]{1,0:T(8,128)S(1)}, f32[256,256]{1,0:T(8,128)S(1)}, u32[]{:S(2)}, u32[]{:S(2)}) collective-permute-start(f32[256,256]{1,0:T(8,128)S(1)} %get-tuple-element.25), channel_id=1, source_target_pairs={{0,1},{1,0},{2,3},{3,2},{4,5},{5,4},{6,7},{7,6},{8,9},{9,8},{10,11... | collective-permute-start | bytes 786440 | tf_op jit(solution)/shard_map/ppermute | solution.py:67
  193.7 2.8 %collective-permute-done.29 = bf16[256,128]{1,0:T(8,128)(2,1)S(1)} collective-permute-done((bf16[256,128]{1,0:T(8,128)(2,1)S(1)}, bf16[256,128]{1,0:T(8,128)(2,1)S(1)}, u32[]{:S(2)}, u32[]{:S(2)}) %collective-permute-start.29) | collective-permute-done | bytes 65568 | tf_op jit(solution)/shard_map/ppermute | solution.py:71
  199.5 3.5 %all-to-all-start.5 = ((bf16[4,4,256,128]{3,2,1,0:T(8,128)(2,1)}), bf16[4,4,256,128]{3,2,1,0:T(8,128)(2,1)S(1)}, u32[]{:S(2)}, u32[]{:S(2)}) async-start(bf16[4,4,256,128]{3,2,1,0:T(8,128)(2,1)} %broadcast_in_dim.26), calls=%async_computation.5 | async-start | bytes 2097152 | tf_op jit(solution)/shard_map/all_to_all | solution.py:84
  203.3 13.6 %all-to-all-done.5.x_ref = bf16[4,4,256,128]{3,2,1,0:T(8,128)(2,1)S(1)} async-done(((bf16[4,4,256,128]{3,2,1,0:T(8,128)(2,1)}), bf16[4,4,256,128]{3,2,1,0:T(8,128)(2,1)S(1)}, u32[]{:S(2)}, u32[]{:S(2)}) %all-to-all-start.5) | async-done | bytes 1048608 | tf_op jit(solution)/shard_map/all_to_all | solution.py:84
  216.9 3.4 %copy-done.3 = bf16[8,2048,256]{2,1,0:T(8,128)(2,1)S(1)} copy-done((bf16[8,2048,256]{2,1,0:T(8,128)(2,1)S(1)}, bf16[8,2048,256]{2,1,0:T(8,128)(2,1)}, u32[]{:S(2)}) %copy-start.3) | copy-done | bytes 8388632
  220.3 2.5 shard_map.73
  231.5 2.6 collective-permute-done.34
  236.5 3.5 %all-to-all-start.6 = ((bf16[4,4,256,128]{3,2,1,0:T(8,128)(2,1)}), bf16[4,4,256,128]{3,2,1,0:T(8,128)(2,1)S(1)}, u32[]{:S(2)}, u32[]{:S(2)}) async-start(bf16[4,4,256,128]{3,2,1,0:T(8,128)(2,1)} %broadcast_in_dim.27), calls=%async_computation.6 | async-start | bytes 2097152 | tf_op jit(solution)/shard_map/all_to_all | solution.py:84
  240.3 12.6 %all-to-all-done.6.x_ref = bf16[4,4,256,128]{3,2,1,0:T(8,128)(2,1)S(1)} async-done(((bf16[4,4,256,128]{3,2,1,0:T(8,128)(2,1)}), bf16[4,4,256,128]{3,2,1,0:T(8,128)(2,1)S(1)}, u32[]{:S(2)}, u32[]{:S(2)}) %all-to-all-start.6) | async-done | bytes 1048608 | tf_op jit(solution)/shard_map/all_to_all | solution.py:84
  252.9 3.4 %copy-done.4 = bf16[8,2048,256]{2,1,0:T(8,128)(2,1)S(1)} copy-done((bf16[8,2048,256]{2,1,0:T(8,128)(2,1)S(1)}, bf16[8,2048,256]{2,1,0:T(8,128)(2,1)}, u32[]{:S(2)}) %copy-start.4) | copy-done | bytes 8388632
  256.2 2.5 shard_map.74
  258.7 3.2 %collective-permute-start.36 = (f32[256,256]{1,0:T(8,128)S(1)}, f32[256,256]{1,0:T(8,128)S(1)}, u32[]{:S(2)}, u32[]{:S(2)}) collective-permute-start(f32[256,256]{1,0:T(8,128)S(1)} %get-tuple-element.29), channel_id=1, source_target_pairs={{0,1},{1,0},{2,3},{3,2},{4,5},{5,4},{6,7},{7,6},{8,9},{9,8},{10,11... | collective-permute-start | bytes 786440 | tf_op jit(solution)/shard_map/ppermute | solution.py:67
  (126 shorter events, 80.7 us)
Async XLA Ops:
  10.0 21.4 %collective-permute-start.4 = (bf16[16,128,8,128]{3,1,0,2:T(8,128)(2,1)}, bf16[16,128,8,128]{3,1,0,2:T(8,128)(2,1)}, u32[]{:S(2)}, u32[]{:S(2)}) collective-permute-start(bf16[16,128,8,128]{3,1,0,2:T(8,128)(2,1)} %bitcast.48), channel_id=1, source_target_pairs={{0,1},{1,0},{2,3},{3,2},{4,5},{5,4},{6,7},{7,6},{8,9},{9,8},{10,11... | collective-permute-start | bytes 12582920 | tf_op jit(solution)/shard_map/ppermute | solution.py:67
  11.4 11.8 %collective-permute-start.3 = (bf16[256,128]{1,0:T(8,128)(2,1)S(1)}, bf16[256,128]{1,0:T(8,128)(2,1)S(1)}, u32[]{:S(2)}, u32[]{:S(2)}) collective-permute-start(bf16[256,128]{1,0:T(8,128)(2,1)S(1)} %slice.99), channel_id=1, source_target_pairs={{0,38},{2,32},{4,34},{6,36},{32,70},{34,64},{36,66},{38,68},{64,10... | collective-permute-start | bytes 196616 | tf_op jit(solution)/shard_map/ppermute | solution.py:71
  15.2 9.2 %collective-permute-start.2 = (bf16[256,128]{1,0:T(8,128)(2,1)S(1)}, bf16[256,128]{1,0:T(8,128)(2,1)S(1)}, u32[]{:S(2)}, u32[]{:S(2)}) collective-permute-start(bf16[256,128]{1,0:T(8,128)(2,1)S(1)} %slice.99), channel_id=1, source_target_pairs={{0,36},{2,38},{4,32},{6,34},{32,68},{34,70},{36,64},{38,66},{64,10... | collective-permute-start | bytes 196616 | tf_op jit(solution)/shard_map/ppermute | solution.py:71
  16.5 7.9 %collective-permute-start.1 = (bf16[256,128]{1,0:T(8,128)(2,1)S(1)}, bf16[256,128]{1,0:T(8,128)(2,1)S(1)}, u32[]{:S(2)}, u32[]{:S(2)}) collective-permute-start(bf16[256,128]{1,0:T(8,128)(2,1)S(1)} %slice.99), channel_id=1, source_target_pairs={{0,34},{2,36},{4,38},{6,32},{32,66},{34,68},{36,70},{38,64},{64,98... | collective-permute-start | bytes 196616 | tf_op jit(solution)/shard_map/ppermute | solution.py:71
  17.8 6.6 %collective-permute-start = (bf16[256,128]{1,0:T(8,128)(2,1)S(1)}, bf16[256,128]{1,0:T(8,128)(2,1)S(1)}, u32[]{:S(2)}, u32[]{:S(2)}) collective-permute-start(bf16[256,128]{1,0:T(8,128)(2,1)S(1)} %slice.99), channel_id=1, source_target_pairs={{0,32},{2,34},{4,36},{6,38},{32,64},{34,66},{36,68},{38,70},{64,96... | collective-permute-start | bytes 196616 | tf_op jit(solution)/shard_map/ppermute | solution.py:71
  23.3 7.4 %collective-permute-start.5 = (f32[8]{0:T(128)S(1)}, f32[8]{0:T(128)S(1)}, u32[]{:S(2)}, u32[]{:S(2)}) collective-permute-start(f32[8]{0:T(128)S(1)} %bitcast.81), channel_id=1, source_target_pairs={{0,1},{1,0},{2,3},{3,2},{4,5},{5,4},{6,7},{7,6},{8,9},{9,8},{10,11... | collective-permute-start | bytes 104 | tf_op jit(solution)/shard_map/ppermute | solution.py:67
  25.7 19.0 %all-to-all-start = ((bf16[4,4,256,128]{3,2,1,0:T(8,128)(2,1)}), bf16[4,4,256,128]{3,2,1,0:T(8,128)(2,1)S(1)}, u32[]{:S(2)}, u32[]{:S(2)}) async-start(bf16[4,4,256,128]{3,2,1,0:T(8,128)(2,1)} %broadcast_in_dim.21), calls=%async_computation | async-start | bytes 2097152 | tf_op jit(solution)/shard_map/all_to_all | solution.py:84
  53.9 6.2 %collective-permute-start.10 = (bf16[256,128]{1,0:T(8,128)(2,1)S(1)}, bf16[256,128]{1,0:T(8,128)(2,1)S(1)}, u32[]{:S(2)}, u32[]{:S(2)}) collective-permute-start(bf16[256,128]{1,0:T(8,128)(2,1)S(1)} %get-tuple-element.47), channel_id=1, source_target_pairs={{0,38},{2,32},{4,34},{6,36},{32,70},{34,64},{36,66},{38,68},{64,10... | collective-permute-start | bytes 196616 | tf_op jit(solution)/shard_map/ppermute | solution.py:71
  56.9 6.7 %collective-permute-start.9 = (bf16[256,128]{1,0:T(8,128)(2,1)S(1)}, bf16[256,128]{1,0:T(8,128)(2,1)S(1)}, u32[]{:S(2)}, u32[]{:S(2)}) collective-permute-start(bf16[256,128]{1,0:T(8,128)(2,1)S(1)} %get-tuple-element.47), channel_id=1, source_target_pairs={{0,36},{2,38},{4,32},{6,34},{32,68},{34,70},{36,64},{38,66},{64,10... | collective-permute-start | bytes 196616 | tf_op jit(solution)/shard_map/ppermute | solution.py:71
  59.2 6.7 %collective-permute-start.8 = (bf16[256,128]{1,0:T(8,128)(2,1)S(1)}, bf16[256,128]{1,0:T(8,128)(2,1)S(1)}, u32[]{:S(2)}, u32[]{:S(2)}) collective-permute-start(bf16[256,128]{1,0:T(8,128)(2,1)S(1)} %get-tuple-element.47), channel_id=1, source_target_pairs={{0,34},{2,36},{4,38},{6,32},{32,66},{34,68},{36,70},{38,64},{64,98... | collective-permute-start | bytes 196616 | tf_op jit(solution)/shard_map/ppermute | solution.py:71
  59.2 6.7 %collective-permute-start.7 = (bf16[256,128]{1,0:T(8,128)(2,1)S(1)}, bf16[256,128]{1,0:T(8,128)(2,1)S(1)}, u32[]{:S(2)}, u32[]{:S(2)}) collective-permute-start(bf16[256,128]{1,0:T(8,128)(2,1)S(1)} %get-tuple-element.47), channel_id=1, source_target_pairs={{0,32},{2,34},{4,36},{6,38},{32,64},{34,66},{36,68},{38,70},{64,96... | collective-permute-start | bytes 196616 | tf_op jit(solution)/shard_map/ppermute | solution.py:71
  92.0 5.3 %collective-permute-start.15 = (bf16[256,128]{1,0:T(8,128)(2,1)S(1)}, bf16[256,128]{1,0:T(8,128)(2,1)S(1)}, u32[]{:S(2)}, u32[]{:S(2)}) collective-permute-start(bf16[256,128]{1,0:T(8,128)(2,1)S(1)} %get-tuple-element.44), channel_id=1, source_target_pairs={{0,38},{2,32},{4,34},{6,36},{32,70},{34,64},{36,66},{38,68},{64,10... | collective-permute-start | bytes 196616 | tf_op jit(solution)/shard_map/ppermute | solution.py:71
  92.5 6.7 %collective-permute-start.14 = (bf16[256,128]{1,0:T(8,128)(2,1)S(1)}, bf16[256,128]{1,0:T(8,128)(2,1)S(1)}, u32[]{:S(2)}, u32[]{:S(2)}) collective-permute-start(bf16[256,128]{1,0:T(8,128)(2,1)S(1)} %get-tuple-element.44), channel_id=1, source_target_pairs={{0,36},{2,38},{4,32},{6,34},{32,68},{34,70},{36,64},{38,66},{64,10... | collective-permute-start | bytes 196616 | tf_op jit(solution)/shard_map/ppermute | solution.py:71
  93.5 7.2 %collective-permute-start.13 = (bf16[256,128]{1,0:T(8,128)(2,1)S(1)}, bf16[256,128]{1,0:T(8,128)(2,1)S(1)}, u32[]{:S(2)}, u32[]{:S(2)}) collective-permute-start(bf16[256,128]{1,0:T(8,128)(2,1)S(1)} %get-tuple-element.44), channel_id=1, source_target_pairs={{0,34},{2,36},{4,38},{6,32},{32,66},{34,68},{36,70},{38,64},{64,98... | collective-permute-start | bytes 196616 | tf_op jit(solution)/shard_map/ppermute | solution.py:71
  94.5 7.4 %collective-permute-start.12 = (bf16[256,128]{1,0:T(8,128)(2,1)S(1)}, bf16[256,128]{1,0:T(8,128)(2,1)S(1)}, u32[]{:S(2)}, u32[]{:S(2)}) collective-permute-start(bf16[256,128]{1,0:T(8,128)(2,1)S(1)} %get-tuple-element.44), channel_id=1, source_target_pairs={{0,32},{2,34},{4,36},{6,38},{32,64},{34,66},{36,68},{38,70},{64,96... | collective-permute-start | bytes 196616 | tf_op jit(solution)/shard_map/ppermute | solution.py:71
  124.4 5.3 %collective-permute-start.20 = (bf16[256,128]{1,0:T(8,128)(2,1)S(1)}, bf16[256,128]{1,0:T(8,128)(2,1)S(1)}, u32[]{:S(2)}, u32[]{:S(2)}) collective-permute-start(bf16[256,128]{1,0:T(8,128)(2,1)S(1)} %get-tuple-element.41), channel_id=1, source_target_pairs={{0,38},{2,32},{4,34},{6,36},{32,70},{34,64},{36,66},{38,68},{64,10... | collective-permute-start | bytes 196616 | tf_op jit(solution)/shard_map/ppermute | solution.py:71
  124.9 6.7 %collective-permute-start.19 = (bf16[256,128]{1,0:T(8,128)(2,1)S(1)}, bf16[256,128]{1,0:T(8,128)(2,1)S(1)}, u32[]{:S(2)}, u32[]{:S(2)}) collective-permute-start(bf16[256,128]{1,0:T(8,128)(2,1)S(1)} %get-tuple-element.41), channel_id=1, source_target_pairs={{0,36},{2,38},{4,32},{6,34},{32,68},{34,70},{36,64},{38,66},{64,10... | collective-permute-start | bytes 196616 | tf_op jit(solution)/shard_map/ppermute | solution.py:71
  126.7 6.8 %collective-permute-start.18 = (bf16[256,128]{1,0:T(8,128)(2,1)S(1)}, bf16[256,128]{1,0:T(8,128)(2,1)S(1)}, u32[]{:S(2)}, u32[]{:S(2)}) collective-permute-start(bf16[256,128]{1,0:T(8,128)(2,1)S(1)} %get-tuple-element.41), channel_id=1, source_target_pairs={{0,34},{2,36},{4,38},{6,32},{32,66},{34,68},{36,70},{38,64},{64,98... | collective-permute-start | bytes 196616 | tf_op jit(solution)/shard_map/ppermute | solution.py:71
  127.8 6.1 %collective-permute-start.17 = (bf16[256,128]{1,0:T(8,128)(2,1)S(1)}, bf16[256,128]{1,0:T(8,128)(2,1)S(1)}, u32[]{:S(2)}, u32[]{:S(2)}) collective-permute-start(bf16[256,128]{1,0:T(8,128)(2,1)S(1)} %get-tuple-element.41), channel_id=1, source_target_pairs={{0,32},{2,34},{4,36},{6,38},{32,64},{34,66},{36,68},{38,70},{64,96... | collective-permute-start | bytes 196616 | tf_op jit(solution)/shard_map/ppermute | solution.py:71
  156.4 5.3 %collective-permute-start.25 = (bf16[256,128]{1,0:T(8,128)(2,1)S(1)}, bf16[256,128]{1,0:T(8,128)(2,1)S(1)}, u32[]{:S(2)}, u32[]{:S(2)}) collective-permute-start(bf16[256,128]{1,0:T(8,128)(2,1)S(1)} %get-tuple-element.38), channel_id=1, source_target_pairs={{0,38},{2,32},{4,34},{6,36},{32,70},{34,64},{36,66},{38,68},{64,10... | collective-permute-start | bytes 196616 | tf_op jit(solution)/shard_map/ppermute | solution.py:71
  157.2 6.9 %collective-permute-start.24 = (bf16[256,128]{1,0:T(8,128)(2,1)S(1)}, bf16[256,128]{1,0:T(8,128)(2,1)S(1)}, u32[]{:S(2)}, u32[]{:S(2)}) collective-permute-start(bf16[256,128]{1,0:T(8,128)(2,1)S(1)} %get-tuple-element.38), channel_id=1, source_target_pairs={{0,36},{2,38},{4,32},{6,34},{32,68},{34,70},{36,64},{38,66},{64,10... | collective-permute-start | bytes 196616 | tf_op jit(solution)/shard_map/ppermute | solution.py:71
  158.5 6.8 %collective-permute-start.23 = (bf16[256,128]{1,0:T(8,128)(2,1)S(1)}, bf16[256,128]{1,0:T(8,128)(2,1)S(1)}, u32[]{:S(2)}, u32[]{:S(2)}) collective-permute-start(bf16[256,128]{1,0:T(8,128)(2,1)S(1)} %get-tuple-element.38), channel_id=1, source_target_pairs={{0,34},{2,36},{4,38},{6,32},{32,66},{34,68},{36,70},{38,64},{64,98... | collective-permute-start | bytes 196616 | tf_op jit(solution)/shard_map/ppermute | solution.py:71
  159.5 5.7 %collective-permute-start.22 = (bf16[256,128]{1,0:T(8,128)(2,1)S(1)}, bf16[256,128]{1,0:T(8,128)(2,1)S(1)}, u32[]{:S(2)}, u32[]{:S(2)}) collective-permute-start(bf16[256,128]{1,0:T(8,128)(2,1)S(1)} %get-tuple-element.38), channel_id=1, source_target_pairs={{0,32},{2,34},{4,36},{6,38},{32,64},{34,66},{36,68},{38,70},{64,96... | collective-permute-start | bytes 196616 | tf_op jit(solution)/shard_map/ppermute | solution.py:71
  187.8 5.9 %collective-permute-start.30 = (bf16[256,128]{1,0:T(8,128)(2,1)S(1)}, bf16[256,128]{1,0:T(8,128)(2,1)S(1)}, u32[]{:S(2)}, u32[]{:S(2)}) collective-permute-start(bf16[256,128]{1,0:T(8,128)(2,1)S(1)} %get-tuple-element.35), channel_id=1, source_target_pairs={{0,38},{2,32},{4,34},{6,36},{32,70},{34,64},{36,66},{38,68},{64,10... | collective-permute-start | bytes 196616 | tf_op jit(solution)/shard_map/ppermute | solution.py:71
  189.6 6.9 %collective-permute-start.29 = (bf16[256,128]{1,0:T(8,128)(2,1)S(1)}, bf16[256,128]{1,0:T(8,128)(2,1)S(1)}, u32[]{:S(2)}, u32[]{:S(2)}) collective-permute-start(bf16[256,128]{1,0:T(8,128)(2,1)S(1)} %get-tuple-element.35), channel_id=1, source_target_pairs={{0,36},{2,38},{4,32},{6,34},{32,68},{34,70},{36,64},{38,66},{64,10... | collective-permute-start | bytes 196616 | tf_op jit(solution)/shard_map/ppermute | solution.py:71
  190.1 7.3 %collective-permute-start.28 = (bf16[256,128]{1,0:T(8,128)(2,1)S(1)}, bf16[256,128]{1,0:T(8,128)(2,1)S(1)}, u32[]{:S(2)}, u32[]{:S(2)}) collective-permute-start(bf16[256,128]{1,0:T(8,128)(2,1)S(1)} %get-tuple-element.35), channel_id=1, source_target_pairs={{0,34},{2,36},{4,38},{6,32},{32,66},{34,68},{36,70},{38,64},{64,98... | collective-permute-start | bytes 196616 | tf_op jit(solution)/shard_map/ppermute | solution.py:71
  191.3 7.0 %collective-permute-start.27 = (bf16[256,128]{1,0:T(8,128)(2,1)S(1)}, bf16[256,128]{1,0:T(8,128)(2,1)S(1)}, u32[]{:S(2)}, u32[]{:S(2)}) collective-permute-start(bf16[256,128]{1,0:T(8,128)(2,1)S(1)} %get-tuple-element.35), channel_id=1, source_target_pairs={{0,32},{2,34},{4,36},{6,38},{32,64},{34,66},{36,68},{38,70},{64,96... | collective-permute-start | bytes 196616 | tf_op jit(solution)/shard_map/ppermute | solution.py:71
  199.5 17.4 %all-to-all-start.5 = ((bf16[4,4,256,128]{3,2,1,0:T(8,128)(2,1)}), bf16[4,4,256,128]{3,2,1,0:T(8,128)(2,1)S(1)}, u32[]{:S(2)}, u32[]{:S(2)}) async-start(bf16[4,4,256,128]{3,2,1,0:T(8,128)(2,1)} %broadcast_in_dim.26), calls=%async_computation.5 | async-start | bytes 2097152 | tf_op jit(solution)/shard_map/all_to_all | solution.py:84
  227.4 6.7 %collective-permute-start.34 = (bf16[256,128]{1,0:T(8,128)(2,1)S(1)}, bf16[256,128]{1,0:T(8,128)(2,1)S(1)}, u32[]{:S(2)}, u32[]{:S(2)}) collective-permute-start(bf16[256,128]{1,0:T(8,128)(2,1)S(1)} %get-tuple-element.32), channel_id=1, source_target_pairs={{0,36},{2,38},{4,32},{6,34},{32,68},{34,70},{36,64},{38,66},{64,10... | collective-permute-start | bytes 196616 | tf_op jit(solution)/shard_map/ppermute | solution.py:71
  228.5 6.7 %collective-permute-start.33 = (bf16[256,128]{1,0:T(8,128)(2,1)S(1)}, bf16[256,128]{1,0:T(8,128)(2,1)S(1)}, u32[]{:S(2)}, u32[]{:S(2)}) collective-permute-start(bf16[256,128]{1,0:T(8,128)(2,1)S(1)} %get-tuple-element.32), channel_id=1, source_target_pairs={{0,34},{2,36},{4,38},{6,32},{32,66},{34,68},{36,70},{38,64},{64,98... | collective-permute-start | bytes 196616 | tf_op jit(solution)/shard_map/ppermute | solution.py:71
  229.6 5.7 %collective-permute-start.32 = (bf16[256,128]{1,0:T(8,128)(2,1)S(1)}, bf16[256,128]{1,0:T(8,128)(2,1)S(1)}, u32[]{:S(2)}, u32[]{:S(2)}) collective-permute-start(bf16[256,128]{1,0:T(8,128)(2,1)S(1)} %get-tuple-element.32), channel_id=1, source_target_pairs={{0,32},{2,34},{4,36},{6,38},{32,64},{34,66},{36,68},{38,70},{64,96... | collective-permute-start | bytes 196616 | tf_op jit(solution)/shard_map/ppermute | solution.py:71
  236.5 16.4 %all-to-all-start.6 = ((bf16[4,4,256,128]{3,2,1,0:T(8,128)(2,1)}), bf16[4,4,256,128]{3,2,1,0:T(8,128)(2,1)S(1)}, u32[]{:S(2)}, u32[]{:S(2)}) async-start(bf16[4,4,256,128]{3,2,1,0:T(8,128)(2,1)} %broadcast_in_dim.27), calls=%async_computation.6 | async-start | bytes 2097152 | tf_op jit(solution)/shard_map/all_to_all | solution.py:84
  (16 other events, 120.9 us)

commit v2 on v1

v2 whole, which is shorter than its diff:
```python
import jax
import jax.numpy as jnp
from jax import lax
from jax.experimental import pallas as pl
from jax.experimental.pallas import tpu as pltpu
from jax.sharding import Mesh, PartitionSpec as P

ROWS = 256
NZ, NY, NC = 4, 4, 2
PLANE = ("z", "y")
BOND = ("z", "y", "core")
VMEM = pl.BlockSpec(memory_space=pltpu.VMEM)
SMEM = pl.BlockSpec(memory_space=pltpu.SMEM)
HBM = pl.BlockSpec(memory_space=pltpu.HBM)


def give_kernel(parity_ref, t_ref, out_ref, held, sems):
    blocks, size = held.shape[:2]
    parity = parity_ref[0]
    copies = [pltpu.make_async_copy(t_ref.at[j, parity], held.at[j], sems.at[j]) for j in range(blocks)]
    for copy in copies:
        copy.start()
    for j in range(blocks):
        copies[j].wait()
        out_ref[:, j * size : (j + 1) * size, :] = jnp.swapaxes(held[j], 0, 1)


def join_kernel(parity_ref, t_ref, got_ref, out_ref, held, sems, got_sem):
    blocks, size = held.shape[:2]
    cols = held.shape[3]
    parity = parity_ref[0]
    copies = [pltpu.make_async_copy(t_ref.at[j, parity], held.at[j], sems.at[j]) for j in range(blocks)]
    for copy in copies:
        copy.start()
    right = pltpu.make_async_copy(got_ref, out_ref.at[:, :, cols:], got_sem)
    right.start()
    for j in range(blocks):
        copies[j].wait()
        out_ref[:, j * size : (j + 1) * size, :cols] = jnp.swapaxes(held[j], 0, 1)
    right.wait()


def give(parity, t):
    blocks, _, size, phys, cols = t.shape
    return pl.pallas_call(
        give_kernel,
        out_shape=jax.ShapeDtypeStruct((phys, blocks * size, cols), t.dtype),
        in_specs=[SMEM, HBM],
        out_specs=VMEM,
        scratch_shapes=[
            pltpu.VMEM((blocks, size, phys, cols), t.dtype),
            pltpu.SemaphoreType.DMA((blocks,)),
        ],
        compiler_params=pltpu.CompilerParams(vmem_limit_bytes=56 * 2**20),
    )(parity, t)


def join(parity, t, got):
    blocks, _, size, phys, cols = t.shape
    return pl.pallas_call(
        join_kernel,
        out_shape=pltpu.VMEM((phys, blocks * size, 2 * cols), t.dtype),
        in_specs=[SMEM, HBM, HBM],
        out_specs=VMEM,
        scratch_shapes=[
            pltpu.VMEM((blocks, size, phys, cols), t.dtype),
            pltpu.SemaphoreType.DMA((blocks,)),
            pltpu.SemaphoreType.DMA,
        ],
        compiler_params=pltpu.CompilerParams(vmem_limit_bytes=48 * 2**20),
    )(parity, t, got)


def contract_kernel(x_ref, w_ref, own_ref, part_ref, mixed_ref, other_ref):
    blocks = [x_ref[j] for j in range(x_ref.shape[0])]
    rows = jnp.concatenate(blocks, axis=1)
    cols = mixed_ref.shape[1]
    squares = None
    for block in blocks:
        wide = block.astype(jnp.float32)
        squares = wide * wide if squares is None else squares + wide * wide
    mixed = jnp.zeros(mixed_ref.shape, jnp.float32)
    other = jnp.zeros(mixed_ref.shape, jnp.float32)
    for p in range(w_ref.shape[0]):
        prod = jnp.dot(rows, w_ref[p], preferred_element_type=jnp.float32)
        mixed += own_ref[:, p : p + 1] * prod[:, :cols]
        other += part_ref[:, p : p + 1] * prod[:, cols:]
    total = jnp.broadcast_to(jnp.sum(squares, axis=1, keepdims=True), mixed_ref.shape)
    mixed_ref[...] = mixed
    other_ref[:, :cols] = other
    other_ref[:, cols:] = total


def contract(x, w, own, part):
    rows, cols = x.shape[1:]
    return pl.pallas_call(
        contract_kernel,
        out_shape=(
            jax.ShapeDtypeStruct((rows, cols), jnp.float32),
            jax.ShapeDtypeStruct((rows, 2 * cols), jnp.float32),
        ),
        in_specs=[VMEM] * 4,
        out_specs=(VMEM, VMEM),
        compiler_params=pltpu.CompilerParams(vmem_limit_bytes=16 * 2**20),
    )(x, w, own, part)


def local(start_rows, site_tensors, block_scales, displacement, outcomes):
    sites = lax.axis_size("site")
    chi, phys, cols = site_tensors.shape[1:]
    allrows = start_rows.shape[0]
    ngroups = allrows // ROWS
    bodies = ngroups + sites - 1
    position = lax.axis_index("site")
    core = lax.axis_index("core")[None].astype(jnp.int32)

    def to_partner(value):
        return lax.ppermute(value, "core", [(0, 1), (1, 0)])

    def ahead(value):
        return lax.ppermute(value, "site", [(s, (s + 1) % sites) for s in range(sites)])

    def plane_gather(value):
        copies = jnp.broadcast_to(value[None], (NZ * NY,) + value.shape)
        return lax.all_to_all(copies, PLANE, 0, 0)

    def start_piece(batch):
        first = min(batch, ngroups - 1) * ROWS
        return start_rows[first : first + ROWS]

    tensor = site_tensors[0].reshape(NZ * NY, NC, cols, phys, cols)
    scale = block_scales[0][:, 0]
    partner_scale = to_partner(scale)
    onehot = (outcomes[0][:, None] == jnp.arange(phys, dtype=jnp.int32)[None, :]).astype(jnp.float32)
    weight = jnp.dot(onehot, displacement[0], precision=lax.Precision.HIGHEST)
    own_coef = weight * scale[None, :]
    part_coef = weight * partner_scale[None, :]
    def coefficients(body):
        first = jnp.clip(body - position, 0, ngroups - 1) * ROWS
        return [lax.dynamic_slice_in_dim(c, first, ROWS, 0) for c in (own_coef, part_coef)]

    coefs = [coefficients(body) for body in range(bodies)]
    sent = give(1 - core, tensor)
    piece, sent, coefs, closing = lax.optimization_barrier(
        (start_piece(0), sent, coefs, position == sites - 1)
    )
    got = to_partner(sent)
    gathered = plane_gather(piece)
    gathered, got = lax.optimization_barrier((gathered, got))
    w = join(core, tensor, got)

    leaves, norms = [], []
    for body in range(bodies):
        mixed, other = contract(gathered, w, *coefs[body])
        arrived = to_partner(other)
        norm = jnp.sqrt((other[:, cols:] + arrived[:, cols:]) / chi + 1e-06)
        leave = ((mixed + arrived[:, :cols]) / norm).astype(jnp.bfloat16)
        if body + 1 < bodies:
            onward = ahead(jnp.where(closing, start_piece(body + 1), leave))
        leaves.append(leave)
        norms.append(norm[:, 0])
        if body + 1 < bodies:
            onward, leaves[-1], norms[-1] = lax.optimization_barrier((onward, leaves[-1], norms[-1]))
            gathered = plane_gather(onward)
    offset = position * ROWS
    out_leave = lax.dynamic_slice_in_dim(jnp.concatenate(leaves, 0), offset, allrows, 0)
    out_norm = lax.dynamic_slice_in_dim(jnp.concatenate(norms, 0), offset, allrows, 0)
    return (out_leave[None], jnp.log(out_norm)[None])


def solution(mesh):
    fine = Mesh(mesh.devices.reshape(-1, NZ, NY, NC), ("site",) + BOND)
    return jax.shard_map(
        local,
        mesh=fine,
        in_specs=(
            P(None, BOND),
            P("site", None, None, BOND),
            P("site", None, BOND),
            P("site", None, None),
            P("site", None),
        ),
        out_specs=(P("site", None, BOND), P("site", None)),
        check_vma=False,
    )
```

time: 265 us -> 226 us (0.85)
  blocking collectives: 62.7 us -> 115 us
  starting transfers between devices: 72.1 us -> 25.5 us
  local copies, waits for them, and re-layouts: 35 us -> 10.2 us
  waiting for transfers between devices: 67.7 us -> 47.4 us
  Pallas kernels: 17.4 us -> 25.3 us
  other arithmetic: 8.54 us -> 0.65 us
    all_to_all x4 -> x6, blocking collectives: 62.7 us -> 115 us  [plane_gather(): return lax.all_to_all(copies, PLANE, 0, 0)]
    ppermute x37 -> x15, starting transfers between devices: 60.1 us -> 21.8 us  [the longest x9 19.9 us: to_partner(): return lax.ppermute(value, 'core', [(0, 1), (1, 0)])]
    all_to_all x3 -> x1, waiting for transfers between devices: 31.8 us -> 15.2 us  [plane_gather(): return lax.all_to_all(copies, PLANE, 0, 0)]
    unnamed x29 -> x26, local copies, waits for them, and re-layouts: 18.9 us -> 5.47 us
    dynamic_slice x4 -> x1, local copies, waits for them, and re-layouts: 10.2 us -> 0.17 us  [coefficients(): lax.dynamic_slice_in_dim(c, first, ROWS, 0)]
    all_to_all x3 -> x1, starting transfers between devices: 12.1 us -> 3.65 us  [plane_gather(): return lax.all_to_all(copies, PLANE, 0, 0)]
    pallas_call x0 -> x2, Pallas kernels: none -> 7.94 us  [the longest x1 4.32 us: give(): pl.pallas_call(give_kernel, out_shape=jax.ShapeDtypeStruct((phys, blocks...]
    concatenate x1 -> x0, other arithmetic: 7.68 us -> none  [local(): jnp.concatenate([jnp.swapaxes(part.reshape(half, phys, cols), 0, 1) for p...]
  transfers between devices with their start and end apart: 40 -> 16, of which waited for: 29 -> 14; matrix products, arithmetic and copies ran while one was open for 6% -> 0% of each run, Pallas kernels for 0% -> 2%
where the time goes in v2:
time: 226 us; the launch traced here: 225 us
  blocking collectives  115 us (51%)
  waiting for transfers between devices  47.4 us (21%)
  starting transfers between devices  25.5 us (11%)
  Pallas kernels  25.3 us (11%)
  local copies, waits for them, and re-layouts  10.2 us (5%)
    all_to_all x6, blocking collectives, plane_gather(): return lax.all_to_all(copies, PLANE, 0, 0)  115 us
    ppermute x6, waiting for transfers between devices, ahead(): lax.ppermute(value, 'site', [(s, (s + 1) % sites) for s in range(sites)])  24 us
    ppermute x9, starting transfers between devices, to_partner(): return lax.ppermute(value, 'core', [(0, 1), (1, 0)])  19.9 us
    pallas_call x7, Pallas kernels, contract(): pl.pallas_call(contract_kernel, out_shape=(jax.ShapeDtypeStruct((rows, co...  17.4 us
    all_to_all x1, waiting for transfers between devices, plane_gather(): return lax.all_to_all(copies, PLANE, 0, 0)  15.2 us
    ppermute x9, waiting for transfers between devices, to_partner(): return lax.ppermute(value, 'core', [(0, 1), (1, 0)])  8.11 us
    unnamed x26, local copies, waits for them, and re-layouts  5.47 us
  transfers between devices with their start and end apart: 16, of which 14 were waited for; matrix products, arithmetic and copies ran while one was open for 0% of the time, Pallas kernels for 2%

profile of v2, /device:TPU:1, one launch (start us, length us, event | category | flops | bytes accessed | tf_op | source)
XLA Modules:
  0.0 225.5 jit_solution(11185010107666973099)
XLA Ops:
  2.2 4.3 %shard_map.68 = bf16[8,2048,128]{2,1,0:T(8,128)(2,1)} custom-call(s32[1]{0:T(128)S(6)} %sub.24.parity_ref, bf16[16,2,128,8,128]{4,3,2,1,0:T(8,128)(2,1)} %bitcast.12), custom_call_target="tpu_custom_call" | custom-call | tf_op jit(solution)/shard_map/pallas_call | solution.py:45
  7.5 23.9 %all_to_all.35.x_ref = bf16[16,256,128]{2,1,0:T(8,128)(2,1)S(1)} all-to-all(bf16[16,256,128]{2,1,0:T(8,128)(2,1)S(1)} %broadcast_in_dim.21), channel_id=1, replica_groups=mesh['site'=4,'z'=4,'y'=4,'core'=2] {'z','y'}, dimensions={0} | all-to-all | bytes 2097152 | tf_op jit(solution)/shard_map/all_to_all | solution.py:125
  31.4 1.9 copy-done.3
  33.4 3.6 %shard_map.69.w_ref = bf16[8,2048,256]{2,1,0:T(8,128)(2,1)S(1)} custom-call(s32[1]{0:T(128)} %bitcast.parity_ref, bf16[16,2,128,8,128]{4,3,2,1,0:T(8,128)(2,1)} %bitcast.13, bf16[8,2048,128]{2,1,0:T(8,128)(2,1)} %copy-done.3), custom_call_target="tpu_custom_call" | custom-call | tf_op jit(solution)/shard_map/pallas_call | solution.py:60
  37.0 2.5 %shard_map.70 = (f32[256,128]{1,0:T(8,128)S(1)}, f32[256,256]{1,0:T(8,128)S(1)}) custom-call(bf16[16,256,128]{2,1,0:T(8,128)(2,1)S(1)} %all_to_all.35.x_ref, bf16[8,2048,256]{2,1,0:T(8,128)(2,1)S(1)} %shard_map.69.w_ref, f32[256,8]{1,0:T(8,128)S(1)} %get-tuple-element.58.own_ref, f32[256,8]{1,0:T(8,128)S(1)} %get-tuple-element.59.part_ref), custom_call_target="tpu_custom_call" | custom-call | tf_op jit(solution)/shard_map/pallas_call | solution.py:96
  39.5 1.9 collective-permute-start.2
  44.1 3.0 %collective-permute-done.3 = bf16[256,128]{1,0:T(8,128)(2,1)S(1)} collective-permute-done((bf16[256,128]{1,0:T(8,128)(2,1)S(1)}, bf16[256,128]{1,0:T(8,128)(2,1)S(1)}, u32[]{:S(2)}, u32[]{:S(2)}) %collective-permute-start.3) | collective-permute-done | bytes 65568 | tf_op jit(solution)/shard_map/ppermute | solution.py:121
  47.3 18.2 %all_to_all.36.x_ref = bf16[16,256,128]{2,1,0:T(8,128)(2,1)S(1)} all-to-all(bf16[16,256,128]{2,1,0:T(8,128)(2,1)S(1)} %broadcast_in_dim.22), channel_id=1, replica_groups=mesh['site'=4,'z'=4,'y'=4,'core'=2] {'z','y'}, dimensions={0} | all-to-all | bytes 2097152 | tf_op jit(solution)/shard_map/all_to_all | solution.py:125
  65.5 2.5 %shard_map.71 = (f32[256,128]{1,0:T(8,128)S(1)}, f32[256,256]{1,0:T(8,128)S(1)}) custom-call(bf16[16,256,128]{2,1,0:T(8,128)(2,1)S(1)} %all_to_all.36.x_ref, bf16[8,2048,256]{2,1,0:T(8,128)(2,1)S(1)} %shard_map.69.w_ref, f32[256,8]{1,0:T(8,128)S(1)} %get-tuple-element.64.own_ref, f32[256,8]{1,0:T(8,128)S(1)} %get-tuple-element.65.part_ref), custom_call_target="tpu_custom_call" | custom-call | tf_op jit(solution)/shard_map/pallas_call | solution.py:96
  67.9 2.7 %collective-permute-start.4 = (f32[256,256]{1,0:T(8,128)S(1)}, f32[256,256]{1,0:T(8,128)S(1)}, u32[]{:S(2)}, u32[]{:S(2)}) collective-permute-start(f32[256,256]{1,0:T(8,128)S(1)} %get-tuple-element.67), channel_id=1, source_target_pairs={{0,1},{1,0},{2,3},{3,2},{4,5},{5,4},{6,7},{7,6},{8,9},{9,8},{10,11... | collective-permute-start | bytes 786440 | tf_op jit(solution)/shard_map/ppermute | solution.py:118
  72.1 4.2 %collective-permute-done.5 = bf16[256,128]{1,0:T(8,128)(2,1)S(1)} collective-permute-done((bf16[256,128]{1,0:T(8,128)(2,1)S(1)}, bf16[256,128]{1,0:T(8,128)(2,1)S(1)}, u32[]{:S(2)}, u32[]{:S(2)}) %collective-permute-start.5) | collective-permute-done | bytes 65568 | tf_op jit(solution)/shard_map/ppermute | solution.py:121
  76.5 18.2 %all_to_all.37.x_ref = bf16[16,256,128]{2,1,0:T(8,128)(2,1)S(1)} all-to-all(bf16[16,256,128]{2,1,0:T(8,128)(2,1)S(1)} %broadcast_in_dim.23), channel_id=1, replica_groups=mesh['site'=4,'z'=4,'y'=4,'core'=2] {'z','y'}, dimensions={0} | all-to-all | bytes 2097152 | tf_op jit(solution)/shard_map/all_to_all | solution.py:125
  94.8 2.5 %shard_map.72 = (f32[256,128]{1,0:T(8,128)S(1)}, f32[256,256]{1,0:T(8,128)S(1)}) custom-call(bf16[16,256,128]{2,1,0:T(8,128)(2,1)S(1)} %all_to_all.37.x_ref, bf16[8,2048,256]{2,1,0:T(8,128)(2,1)S(1)} %shard_map.69.w_ref, f32[256,8]{1,0:T(8,128)S(1)} %get-tuple-element.70.own_ref, f32[256,8]{1,0:T(8,128)S(1)} %get-tuple-element.71.part_ref), custom_call_target="tpu_custom_call" | custom-call | tf_op jit(solution)/shard_map/pallas_call | solution.py:96
  97.3 2.7 %collective-permute-start.6 = (f32[256,256]{1,0:T(8,128)S(1)}, f32[256,256]{1,0:T(8,128)S(1)}, u32[]{:S(2)}, u32[]{:S(2)}) collective-permute-start(f32[256,256]{1,0:T(8,128)S(1)} %get-tuple-element.73), channel_id=1, source_target_pairs={{0,1},{1,0},{2,3},{3,2},{4,5},{5,4},{6,7},{7,6},{8,9},{9,8},{10,11... | collective-permute-start | bytes 786440 | tf_op jit(solution)/shard_map/ppermute | solution.py:118
  101.4 4.2 %collective-permute-done.7 = bf16[256,128]{1,0:T(8,128)(2,1)S(1)} collective-permute-done((bf16[256,128]{1,0:T(8,128)(2,1)S(1)}, bf16[256,128]{1,0:T(8,128)(2,1)S(1)}, u32[]{:S(2)}, u32[]{:S(2)}) %collective-permute-start.7) | collective-permute-done | bytes 65568 | tf_op jit(solution)/shard_map/ppermute | solution.py:121
  105.8 18.3 %all_to_all.38.x_ref = bf16[16,256,128]{2,1,0:T(8,128)(2,1)S(1)} all-to-all(bf16[16,256,128]{2,1,0:T(8,128)(2,1)S(1)} %broadcast_in_dim.24), channel_id=1, replica_groups=mesh['site'=4,'z'=4,'y'=4,'core'=2] {'z','y'}, dimensions={0} | all-to-all | bytes 2097152 | tf_op jit(solution)/shard_map/all_to_all | solution.py:125
  124.0 2.5 %shard_map.73 = (f32[256,128]{1,0:T(8,128)S(1)}, f32[256,256]{1,0:T(8,128)S(1)}) custom-call(bf16[16,256,128]{2,1,0:T(8,128)(2,1)S(1)} %all_to_all.38.x_ref, bf16[8,2048,256]{2,1,0:T(8,128)(2,1)S(1)} %shard_map.69.w_ref, f32[256,8]{1,0:T(8,128)S(1)} %get-tuple-element.76.own_ref, f32[256,8]{1,0:T(8,128)S(1)} %get-tuple-element.77.part_ref), custom_call_target="tpu_custom_call" | custom-call | tf_op jit(solution)/shard_map/pallas_call | solution.py:96
  126.5 2.6 %collective-permute-start.8 = (f32[256,256]{1,0:T(8,128)S(1)}, f32[256,256]{1,0:T(8,128)S(1)}, u32[]{:S(2)}, u32[]{:S(2)}) collective-permute-start(f32[256,256]{1,0:T(8,128)S(1)} %get-tuple-element.79), channel_id=1, source_target_pairs={{0,1},{1,0},{2,3},{3,2},{4,5},{5,4},{6,7},{7,6},{8,9},{9,8},{10,11... | collective-permute-start | bytes 786440 | tf_op jit(solution)/shard_map/ppermute | solution.py:118
  130.6 4.2 %collective-permute-done.9 = bf16[256,128]{1,0:T(8,128)(2,1)S(1)} collective-permute-done((bf16[256,128]{1,0:T(8,128)(2,1)S(1)}, bf16[256,128]{1,0:T(8,128)(2,1)S(1)}, u32[]{:S(2)}, u32[]{:S(2)}) %collective-permute-start.9) | collective-permute-done | bytes 65568 | tf_op jit(solution)/shard_map/ppermute | solution.py:121
  135.0 18.2 %all_to_all.39.x_ref = bf16[16,256,128]{2,1,0:T(8,128)(2,1)S(1)} all-to-all(bf16[16,256,128]{2,1,0:T(8,128)(2,1)S(1)} %broadcast_in_dim.25), channel_id=1, replica_groups=mesh['site'=4,'z'=4,'y'=4,'core'=2] {'z','y'}, dimensions={0} | all-to-all | bytes 2097152 | tf_op jit(solution)/shard_map/all_to_all | solution.py:125
  153.2 2.5 %shard_map.74 = (f32[256,128]{1,0:T(8,128)S(1)}, f32[256,256]{1,0:T(8,128)S(1)}) custom-call(bf16[16,256,128]{2,1,0:T(8,128)(2,1)S(1)} %all_to_all.39.x_ref, bf16[8,2048,256]{2,1,0:T(8,128)(2,1)S(1)} %shard_map.69.w_ref, f32[256,8]{1,0:T(8,128)S(1)} %get-tuple-element.82.own_ref, f32[256,8]{1,0:T(8,128)S(1)} %get-tuple-element.83.part_ref), custom_call_target="tpu_custom_call" | custom-call | tf_op jit(solution)/shard_map/pallas_call | solution.py:96
  155.7 2.6 %collective-permute-start.10 = (f32[256,256]{1,0:T(8,128)S(1)}, f32[256,256]{1,0:T(8,128)S(1)}, u32[]{:S(2)}, u32[]{:S(2)}) collective-permute-start(f32[256,256]{1,0:T(8,128)S(1)} %get-tuple-element.85), channel_id=1, source_target_pairs={{0,1},{1,0},{2,3},{3,2},{4,5},{5,4},{6,7},{7,6},{8,9},{9,8},{10,11... | collective-permute-start | bytes 786440 | tf_op jit(solution)/shard_map/ppermute | solution.py:118
  159.8 4.2 %collective-permute-done.11 = bf16[256,128]{1,0:T(8,128)(2,1)S(1)} collective-permute-done((bf16[256,128]{1,0:T(8,128)(2,1)S(1)}, bf16[256,128]{1,0:T(8,128)(2,1)S(1)}, u32[]{:S(2)}, u32[]{:S(2)}) %collective-permute-start.11) | collective-permute-done | bytes 65568 | tf_op jit(solution)/shard_map/ppermute | solution.py:121
  164.2 18.2 %all_to_all.40.x_ref = bf16[16,256,128]{2,1,0:T(8,128)(2,1)S(1)} all-to-all(bf16[16,256,128]{2,1,0:T(8,128)(2,1)S(1)} %broadcast_in_dim.26), channel_id=1, replica_groups=mesh['site'=4,'z'=4,'y'=4,'core'=2] {'z','y'}, dimensions={0} | all-to-all | bytes 2097152 | tf_op jit(solution)/shard_map/all_to_all | solution.py:125
  182.4 2.5 %shard_map.75 = (f32[256,128]{1,0:T(8,128)S(1)}, f32[256,256]{1,0:T(8,128)S(1)}) custom-call(bf16[16,256,128]{2,1,0:T(8,128)(2,1)S(1)} %all_to_all.40.x_ref, bf16[8,2048,256]{2,1,0:T(8,128)(2,1)S(1)} %shard_map.69.w_ref, f32[256,8]{1,0:T(8,128)S(1)} %get-tuple-element.88.own_ref, f32[256,8]{1,0:T(8,128)S(1)} %get-tuple-element.89.part_ref), custom_call_target="tpu_custom_call" | custom-call | tf_op jit(solution)/shard_map/pallas_call | solution.py:96
  184.9 2.6 %collective-permute-start.12 = (f32[256,256]{1,0:T(8,128)S(1)}, f32[256,256]{1,0:T(8,128)S(1)}, u32[]{:S(2)}, u32[]{:S(2)}) collective-permute-start(f32[256,256]{1,0:T(8,128)S(1)} %get-tuple-element.91), channel_id=1, source_target_pairs={{0,1},{1,0},{2,3},{3,2},{4,5},{5,4},{6,7},{7,6},{8,9},{9,8},{10,11... | collective-permute-start | bytes 786440 | tf_op jit(solution)/shard_map/ppermute | solution.py:118
  189.2 4.2 %collective-permute-done.13 = bf16[256,128]{1,0:T(8,128)(2,1)S(1)} collective-permute-done((bf16[256,128]{1,0:T(8,128)(2,1)S(1)}, bf16[256,128]{1,0:T(8,128)(2,1)S(1)}, u32[]{:S(2)}, u32[]{:S(2)}) %collective-permute-start.13) | collective-permute-done | bytes 65568 | tf_op jit(solution)/shard_map/ppermute | solution.py:121
  194.7 3.7 %all-to-all-start.6 = ((bf16[16,256,128]{2,1,0:T(8,128)(2,1)}), bf16[16,256,128]{2,1,0:T(8,128)(2,1)S(1)}, u32[]{:S(2)}, u32[]{:S(2)}) async-start(bf16[16,256,128]{2,1,0:T(8,128)(2,1)} %broadcast_in_dim.27), calls=%async_computation.6 | async-start | bytes 2097152 | tf_op jit(solution)/shard_map/all_to_all | solution.py:125
  198.5 15.2 %all-to-all-done.6.x_ref = bf16[16,256,128]{2,1,0:T(8,128)(2,1)S(1)} async-done(((bf16[16,256,128]{2,1,0:T(8,128)(2,1)}), bf16[16,256,128]{2,1,0:T(8,128)(2,1)S(1)}, u32[]{:S(2)}, u32[]{:S(2)}) %all-to-all-start.6) | async-done | bytes 1048608 | tf_op jit(solution)/shard_map/all_to_all | solution.py:125
  213.7 3.4 %copy-done.2 = bf16[8,2048,256]{2,1,0:T(8,128)(2,1)S(1)} copy-done((bf16[8,2048,256]{2,1,0:T(8,128)(2,1)S(1)}, bf16[8,2048,256]{2,1,0:T(8,128)(2,1)}, u32[]{:S(2)}) %copy-start.2) | copy-done | bytes 8388632
  217.1 2.5 %shard_map.76 = (f32[256,128]{1,0:T(8,128)S(1)}, f32[256,256]{1,0:T(8,128)S(1)}) custom-call(bf16[16,256,128]{2,1,0:T(8,128)(2,1)S(1)} %all-to-all-done.6.x_ref, bf16[8,2048,256]{2,1,0:T(8,128)(2,1)S(1)} %copy-done.2, f32[256,8]{1,0:T(8,128)S(1)} %get-tuple-element.94.own_ref, f32[256,8]{1,0:T(8,128)S(1)} %get-tuple-element.95.part_ref), custom_call_target="tpu_custom_call" | custom-call | tf_op jit(solution)/shard_map/pallas_call | solution.py:96
  219.6 3.1 %collective-permute-start.14 = (f32[256,256]{1,0:T(8,128)S(1)}, f32[256,256]{1,0:T(8,128)S(1)}, u32[]{:S(2)}, u32[]{:S(2)}) collective-permute-start(f32[256,256]{1,0:T(8,128)S(1)} %get-tuple-element.97), channel_id=1, source_target_pairs={{0,1},{1,0},{2,3},{3,2},{4,5},{5,4},{6,7},{7,6},{8,9},{9,8},{10,11... | collective-permute-start | bytes 786440 | tf_op jit(solution)/shard_map/ppermute | solution.py:118
  (70 shorter events, 17.6 us)
Async XLA Ops:
  0.6 5.9 %copy-start = (f32[1,8,8]{2,1,0:T(8,128)S(1)}, f32[1,8,8]{2,1,0:T(8,128)}, u32[]{:S(2)}) copy-start(f32[1,8,8]{2,1,0:T(8,128)} %param.8) | copy-start | bytes 772
  0.6 5.9 %copy-start.6 = (f32[1,8,1]{1,2,0:T(1,128)S(1)}, f32[1,8,1]{1,2,0:T(1,128)}, u32[]{:S(2)}) copy-start(f32[1,8,1]{1,2,0:T(1,128)} %param.7) | copy-start | bytes 100
  0.7 5.9 %copy-start.5 = (s32[1,1024]{1,0:T(1,128)S(1)}, s32[1,1024]{1,0:T(1,128)}, u32[]{:S(2)}) copy-start(s32[1,1024]{1,0:T(1,128)} %param.9) | copy-start | bytes 12292
  0.7 5.8 %collective-permute-start = (f32[8]{0:T(128)}, f32[8]{0:T(128)S(1)}, u32[]{:S(2)}, u32[]{:S(2)}) collective-permute-start(f32[8]{0:T(128)} %bitcast.16), channel_id=1, source_target_pairs={{0,1},{1,0},{2,3},{3,2},{4,5},{5,4},{6,7},{7,6},{8,9},{9,8},{10,11... | collective-permute-start | bytes 104 | tf_op jit(solution)/shard_map/ppermute | solution.py:118
  2.2 5.2 %slice-start = ((bf16[1024,128]{1,0:T(8,128)(2,1)}), bf16[256,128]{1,0:T(8,128)(2,1)S(1)}, s32[]{:S(2)}) async-start(bf16[1024,128]{1,0:T(8,128)(2,1)} %param.5), calls=%async_computation.7 | async-start | bytes 131072 | tf_op jit(solution)/shard_map/slice | solution.py:129
  7.2 24.2 %collective-permute-start.1 = (bf16[8,2048,128]{2,1,0:T(8,128)(2,1)}, bf16[8,2048,128]{2,1,0:T(8,128)(2,1)S(1)}, u32[]{:S(2)}, u32[]{:S(2)}) collective-permute-start(bf16[8,2048,128]{2,1,0:T(8,128)(2,1)} %shard_map.68), channel_id=1, source_target_pairs={{0,1},{1,0},{2,3},{3,2},{4,5},{5,4},{6,7},{7,6},{8,9},{9,8},{10,11... | collective-permute-start | bytes 12582920 | tf_op jit(solution)/shard_map/ppermute | solution.py:118
  31.4 1.9 copy-start.3
  37.0 145.5 %copy-start.1 = (bf16[8,2048,256]{2,1,0:T(8,128)(2,1)}, bf16[8,2048,256]{2,1,0:T(8,128)(2,1)S(1)}, u32[]{:S(2)}) copy-start(bf16[8,2048,256]{2,1,0:T(8,128)(2,1)S(1)} %shard_map.69.w_ref) | copy-start | bytes 25165828
  37.0 5.6 %copy-start.4 = (bf16[1024,128]{1,0:T(8,128)(2,1)S(1)}, bf16[1024,128]{1,0:T(8,128)(2,1)}, u32[]{:S(2)}) copy-start(bf16[1024,128]{1,0:T(8,128)(2,1)} %param.5) | copy-start | bytes 786436
  39.5 3.1 %collective-permute-start.2 = (f32[256,256]{1,0:T(8,128)S(1)}, f32[256,256]{1,0:T(8,128)S(1)}, u32[]{:S(2)}, u32[]{:S(2)}) collective-permute-start(f32[256,256]{1,0:T(8,128)S(1)} %get-tuple-element.61), channel_id=1, source_target_pairs={{0,1},{1,0},{2,3},{3,2},{4,5},{5,4},{6,7},{7,6},{8,9},{9,8},{10,11... | collective-permute-start | bytes 786440 | tf_op jit(solution)/shard_map/ppermute | solution.py:118
  42.7 4.4 %collective-permute-start.3 = (bf16[256,128]{1,0:T(8,128)(2,1)S(1)}, bf16[256,128]{1,0:T(8,128)(2,1)S(1)}, u32[]{:S(2)}, u32[]{:S(2)}) collective-permute-start(bf16[256,128]{1,0:T(8,128)(2,1)S(1)} %get-tuple-element.121), channel_id=1, source_target_pairs={{0,32},{32,64},{64,96},{96,0},{1,33},{33,65},{65,97},{97,1},{2,34}... | collective-permute-start | bytes 196616 | tf_op jit(solution)/shard_map/ppermute | solution.py:121
  67.9 3.9 %collective-permute-start.4 = (f32[256,256]{1,0:T(8,128)S(1)}, f32[256,256]{1,0:T(8,128)S(1)}, u32[]{:S(2)}, u32[]{:S(2)}) collective-permute-start(f32[256,256]{1,0:T(8,128)S(1)} %get-tuple-element.67), channel_id=1, source_target_pairs={{0,1},{1,0},{2,3},{3,2},{4,5},{5,4},{6,7},{7,6},{8,9},{9,8},{10,11... | collective-permute-start | bytes 786440 | tf_op jit(solution)/shard_map/ppermute | solution.py:118
  72.0 4.4 %collective-permute-start.5 = (bf16[256,128]{1,0:T(8,128)(2,1)S(1)}, bf16[256,128]{1,0:T(8,128)(2,1)S(1)}, u32[]{:S(2)}, u32[]{:S(2)}) collective-permute-start(bf16[256,128]{1,0:T(8,128)(2,1)S(1)} %get-tuple-element.118), channel_id=1, source_target_pairs={{0,32},{32,64},{64,96},{96,0},{1,33},{33,65},{65,97},{97,1},{2,34}... | collective-permute-start | bytes 196616 | tf_op jit(solution)/shard_map/ppermute | solution.py:121
  97.3 3.8 %collective-permute-start.6 = (f32[256,256]{1,0:T(8,128)S(1)}, f32[256,256]{1,0:T(8,128)S(1)}, u32[]{:S(2)}, u32[]{:S(2)}) collective-permute-start(f32[256,256]{1,0:T(8,128)S(1)} %get-tuple-element.73), channel_id=1, source_target_pairs={{0,1},{1,0},{2,3},{3,2},{4,5},{5,4},{6,7},{7,6},{8,9},{9,8},{10,11... | collective-permute-start | bytes 786440 | tf_op jit(solution)/shard_map/ppermute | solution.py:118
  101.2 4.4 %collective-permute-start.7 = (bf16[256,128]{1,0:T(8,128)(2,1)S(1)}, bf16[256,128]{1,0:T(8,128)(2,1)S(1)}, u32[]{:S(2)}, u32[]{:S(2)}) collective-permute-start(bf16[256,128]{1,0:T(8,128)(2,1)S(1)} %get-tuple-element.115), channel_id=1, source_target_pairs={{0,32},{32,64},{64,96},{96,0},{1,33},{33,65},{65,97},{97,1},{2,34}... | collective-permute-start | bytes 196616 | tf_op jit(solution)/shard_map/ppermute | solution.py:121
  126.5 3.8 %collective-permute-start.8 = (f32[256,256]{1,0:T(8,128)S(1)}, f32[256,256]{1,0:T(8,128)S(1)}, u32[]{:S(2)}, u32[]{:S(2)}) collective-permute-start(f32[256,256]{1,0:T(8,128)S(1)} %get-tuple-element.79), channel_id=1, source_target_pairs={{0,1},{1,0},{2,3},{3,2},{4,5},{5,4},{6,7},{7,6},{8,9},{9,8},{10,11... | collective-permute-start | bytes 786440 | tf_op jit(solution)/shard_map/ppermute | solution.py:118
  130.4 4.4 %collective-permute-start.9 = (bf16[256,128]{1,0:T(8,128)(2,1)S(1)}, bf16[256,128]{1,0:T(8,128)(2,1)S(1)}, u32[]{:S(2)}, u32[]{:S(2)}) collective-permute-start(bf16[256,128]{1,0:T(8,128)(2,1)S(1)} %get-tuple-element.112), channel_id=1, source_target_pairs={{0,32},{32,64},{64,96},{96,0},{1,33},{33,65},{65,97},{97,1},{2,34}... | collective-permute-start | bytes 196616 | tf_op jit(solution)/shard_map/ppermute | solution.py:121
  155.7 3.8 %collective-permute-start.10 = (f32[256,256]{1,0:T(8,128)S(1)}, f32[256,256]{1,0:T(8,128)S(1)}, u32[]{:S(2)}, u32[]{:S(2)}) collective-permute-start(f32[256,256]{1,0:T(8,128)S(1)} %get-tuple-element.85), channel_id=1, source_target_pairs={{0,1},{1,0},{2,3},{3,2},{4,5},{5,4},{6,7},{7,6},{8,9},{9,8},{10,11... | collective-permute-start | bytes 786440 | tf_op jit(solution)/shard_map/ppermute | solution.py:118
  159.6 4.4 %collective-permute-start.11 = (bf16[256,128]{1,0:T(8,128)(2,1)S(1)}, bf16[256,128]{1,0:T(8,128)(2,1)S(1)}, u32[]{:S(2)}, u32[]{:S(2)}) collective-permute-start(bf16[256,128]{1,0:T(8,128)(2,1)S(1)} %get-tuple-element.109), channel_id=1, source_target_pairs={{0,32},{32,64},{64,96},{96,0},{1,33},{33,65},{65,97},{97,1},{2,34}... | collective-permute-start | bytes 196616 | tf_op jit(solution)/shard_map/ppermute | solution.py:121
  184.9 3.8 %collective-permute-start.12 = (f32[256,256]{1,0:T(8,128)S(1)}, f32[256,256]{1,0:T(8,128)S(1)}, u32[]{:S(2)}, u32[]{:S(2)}) collective-permute-start(f32[256,256]{1,0:T(8,128)S(1)} %get-tuple-element.91), channel_id=1, source_target_pairs={{0,1},{1,0},{2,3},{3,2},{4,5},{5,4},{6,7},{7,6},{8,9},{9,8},{10,11... | collective-permute-start | bytes 786440 | tf_op jit(solution)/shard_map/ppermute | solution.py:118
  188.8 4.6 %collective-permute-start.13 = (bf16[256,128]{1,0:T(8,128)(2,1)S(1)}, bf16[256,128]{1,0:T(8,128)(2,1)S(1)}, u32[]{:S(2)}, u32[]{:S(2)}) collective-permute-start(bf16[256,128]{1,0:T(8,128)(2,1)S(1)} %get-tuple-element.106), channel_id=1, source_target_pairs={{0,32},{32,64},{64,96},{96,0},{1,33},{33,65},{65,97},{97,1},{2,34}... | collective-permute-start | bytes 196616 | tf_op jit(solution)/shard_map/ppermute | solution.py:121
  194.7 19.0 %all-to-all-start.6 = ((bf16[16,256,128]{2,1,0:T(8,128)(2,1)}), bf16[16,256,128]{2,1,0:T(8,128)(2,1)S(1)}, u32[]{:S(2)}, u32[]{:S(2)}) async-start(bf16[16,256,128]{2,1,0:T(8,128)(2,1)} %broadcast_in_dim.27), calls=%async_computation.6 | async-start | bytes 2097152 | tf_op jit(solution)/shard_map/all_to_all | solution.py:125
  213.7 3.4 %copy-start.2 = (bf16[8,2048,256]{2,1,0:T(8,128)(2,1)S(1)}, bf16[8,2048,256]{2,1,0:T(8,128)(2,1)}, u32[]{:S(2)}) copy-start(bf16[8,2048,256]{2,1,0:T(8,128)(2,1)} %copy-done.1) | copy-start | bytes 25165828
  219.6 4.2 %collective-permute-start.14 = (f32[256,256]{1,0:T(8,128)S(1)}, f32[256,256]{1,0:T(8,128)S(1)}, u32[]{:S(2)}, u32[]{:S(2)}) collective-permute-start(f32[256,256]{1,0:T(8,128)S(1)} %get-tuple-element.97), channel_id=1, source_target_pairs={{0,1},{1,0},{2,3},{3,2},{4,5},{5,4},{6,7},{7,6},{8,9},{9,8},{10,11... | collective-permute-start | bytes 786440 | tf_op jit(solution)/shard_map/ppermute | solution.py:118
